TPU v7x, 256 devices: a whole 4x4x8 slice. The times are simulated.
256 devices in a mesh: outer: 32 (over z, y), inner: 8 (over x, core).
Axes of the slice: x: 4, y: 4, z: 8, core: 2. Of those that a mesh axis runs over, the one named last changes fastest.
Arguments:
- based_query: bfloat16 [32768, 110], P(('outer', 'inner')), may hold values from -5 to 5
- based_key: bfloat16 [32768, 110], P(('outer', 'inner')), may hold values from -5 to 5
- based_value: bfloat16 [32768, 640], P(('outer', 'inner')), may hold values from -6 to 6
- norm_gain: float32 [640], replicated, may hold values from 0.1 to 1.9
- doc_ids: int32 [32768], P(('outer', 'inner')), may hold values from 0 to 15, never falling along the last dimension, each value on 1 to 8192 neighbouring positions
- window_query: bfloat16 [32768, 1280], P(('outer', 'inner')), may hold values from -4.5 to 4.5
- window_key: bfloat16 [32768, 1280], P(('outer', 'inner')), may hold values from -4.5 to 4.5
- window_value: bfloat16 [32768, 1280], P(('outer', 'inner')), may hold values from -6 to 6
Outputs:
- based_out: bfloat16 [32768, 640], P(('outer', 'inner'))
- window_out: bfloat16 [32768, 1280], P(('outer', 'inner'))
All inputs are finite; a program needn't handle non-finite values.
Results may differ from a plain program's by a relative error of at most 0.004.
Values may be sent and summed in bfloat16 or wider, within the bound.
A program may use at most 320 MiB of HBM per device.

v0:
```python
import math

import jax
import jax.numpy as jnp
from jax import lax
from jax.sharding import PartitionSpec as P

HEADS = 10
BASED_DIM = 64
HEAD_DIM = 128
QK_DIM = 11
WIN_HEADS = 10
WINDOW = 1024
FEATURES = 144


def entering(part, axis, combine, identity):
    place = lax.axis_index(axis)
    gathered = jax.tree.map(lambda a: lax.all_gather(a, axis), part)
    state = jax.tree.map(lambda a, e: jnp.zeros_like(a) + jnp.asarray(e, a.dtype), part, identity)

    def one(step, state):
        return combine(
            state, jax.tree.map(lambda a: lax.dynamic_index_in_dim(a, step, 0, False), gathered)
        )

    return lax.fori_loop(0, place, one, state)


def broadcast(block, axis, source):
    block = jnp.where(lax.axis_index(axis) == source, block, jnp.zeros_like(block))
    return lax.psum(block, axis)


def shifted(block, axis, distance):
    devices = range(lax.axis_size(axis))
    route = [(i - distance, i) for i in devices if i - distance in devices]
    return lax.ppermute(block, axis, route)


def lift_cols(proj):
    rows = proj.shape[0]
    half = proj.astype(jnp.float32).T.reshape(HEADS, QK_DIM, rows) * 0.5
    ones = jnp.ones((HEADS, 1, rows), jnp.float32)
    return jnp.concatenate([ones, half], axis=1)


def feature_cols(lifted):
    rows = lifted.shape[2]
    outer = lifted[:, :, None, :] * lifted[:, None, :, :]
    return outer.reshape(HEADS, FEATURES, rows).astype(jnp.bfloat16)


def combine_state(earlier, later):
    state_a, last_a, begin_a = earlier
    state_b, last_b, begin_b = later
    empty_b = last_b < 0.0
    same = last_a == last_b
    state = jnp.where(empty_b, state_a, state_b + jnp.where(same, state_a, 0.0))
    last = jnp.where(empty_b, last_a, last_b)
    begin = jnp.where(empty_b, begin_a, jnp.where(same, begin_a, begin_b))
    return (state, last, begin)


def body(
    based_query, based_key, based_value, norm_gain, doc_ids, window_query, window_key, window_value
):
    rows = based_query.shape[0]
    here = lax.axis_index(("outer", "inner"))
    offset = here * rows
    positions = offset + jnp.arange(rows, dtype=jnp.int32)
    lifted_q = lift_cols(based_query)
    lifted_k = lift_cols(based_key)
    feat_k = feature_cols(lifted_k)
    values_t = based_value.T.reshape(HEADS, BASED_DIM, rows)
    last_doc = doc_ids[rows - 1]
    keep = doc_ids == last_doc
    local = jnp.einsum(
        "hft,hdt->hfd",
        feat_k * keep.astype(jnp.bfloat16)[None, None, :],
        values_t,
        preferred_element_type=jnp.float32,
    )
    begin = jnp.min(jnp.where(keep, positions, offset + rows)).astype(jnp.float32)
    element = (local, last_doc.astype(jnp.float32), begin)
    identity = (jnp.zeros_like(local), jnp.float32(-1.0), jnp.float32(0.0))
    inner_part = entering(element, "inner", combine_state, identity)
    inclusive = combine_state(inner_part, element)
    group_state = (
        broadcast(inclusive[0], "inner", lax.axis_size("inner") - 1),
        broadcast(inclusive[1], "inner", lax.axis_size("inner") - 1),
        broadcast(inclusive[2], "inner", lax.axis_size("inner") - 1),
    )
    outer_part = entering(group_state, "outer", combine_state, identity)
    prefix = combine_state(outer_part, inner_part)
    prefix_state, prefix_last, prefix_begin = prefix
    carried = doc_ids.astype(jnp.float32) == prefix_last
    feat_q = feature_cols(lifted_q)
    inter = jnp.einsum(
        "hft,hfd->hdt", feat_q.astype(jnp.float32), prefix_state, precision=lax.Precision.HIGHEST
    )
    inter = inter * carried.astype(jnp.float32)[None, None, :]
    kernel = jnp.einsum("hpi,hpj->hij", lifted_q, lifted_k, precision=lax.Precision.HIGHEST) ** 2
    same_doc = doc_ids[None, :] == doc_ids[:, None]
    causal = positions[None, :] <= positions[:, None]
    weights = jnp.where((same_doc & causal)[None], kernel, 0.0).astype(jnp.bfloat16)
    intra = jnp.einsum("hij,hdj->hdi", weights, values_t, preferred_element_type=jnp.float32)
    total = inter + intra
    normed = total * lax.rsqrt(jnp.mean(total * total, axis=1, keepdims=True) + 1e-05)
    scaled = normed * norm_gain.reshape(HEADS, BASED_DIM, 1)
    based_out = scaled.astype(jnp.bfloat16).reshape(HEADS * BASED_DIM, rows).T
    first_local = jnp.min(jnp.where(same_doc, positions[None, :], offset + rows), axis=1)
    doc_begin = jnp.where(carried, prefix_begin.astype(jnp.int32), first_local)
    reach = WINDOW // rows
    key_parts = []
    value_parts = []
    for back in range(reach, 0, -1):
        moved_key, moved_value = shifted((window_key, window_value), ("outer", "inner"), back)
        key_parts.append(moved_key)
        value_parts.append(moved_value)
    keys_all = jnp.concatenate(key_parts + [window_key], axis=0)
    values_all = jnp.concatenate(value_parts + [window_value], axis=0)
    key_pos = offset - reach * rows + jnp.arange(rows * (reach + 1), dtype=jnp.int32)
    visible = (
        (key_pos[None, :] <= positions[:, None])
        & (key_pos[None, :] > positions[:, None] - WINDOW)
        & (key_pos[None, :] >= doc_begin[:, None])
    )
    scale = 1.0 / math.sqrt(HEAD_DIM)

    def one_head(head):
        start = head * HEAD_DIM
        query_head = lax.dynamic_slice_in_dim(window_query, start, HEAD_DIM, 1)
        key_head = lax.dynamic_slice_in_dim(keys_all, start, HEAD_DIM, 1)
        value_head = lax.dynamic_slice_in_dim(values_all, start, HEAD_DIM, 1)
        scores = (
            jnp.einsum("ad,bd->ab", query_head, key_head, preferred_element_type=jnp.float32)
            * scale
        )
        scores = jnp.where(visible, scores, -1e30)
        top = jnp.max(scores, axis=1, keepdims=True)
        probs = jnp.exp(scores - top)
        rowsum = jnp.sum(probs, axis=1, keepdims=True)
        mixed = (
            jnp.dot(probs.astype(jnp.bfloat16), value_head, preferred_element_type=jnp.float32)
            / rowsum
        )
        return mixed.astype(jnp.bfloat16)

    per_head = lax.map(one_head, jnp.arange(WIN_HEADS, dtype=jnp.int32))
    window_out = per_head.transpose(1, 0, 2).reshape(rows, WIN_HEADS * HEAD_DIM)
    return (based_out, window_out)


def solution(mesh):
    placed = (
        P(("outer", "inner"), None),
        P(("outer", "inner"), None),
        P(("outer", "inner"), None),
        P(),
        P(("outer", "inner")),
        P(("outer", "inner"), None),
        P(("outer", "inner"), None),
        P(("outer", "inner"), None),
    )
    return jax.shard_map(
        body,
        mesh=mesh,
        in_specs=placed,
        out_specs=(P(("outer", "inner"), None), P(("outer", "inner"), None)),
        check_vma=False,
    )
```

profile of v0, /device:TPU:255, one launch (start us, length us, event | category | flops | bytes accessed | tf_op | source)
XLA Modules:
  0.0 624.3 jit_solution(14804007272479219266)
XLA Ops:
  7.2 1.3 slice.3
  8.5 1.3 compare_convert_fusion.1
  11.9 1.3 fusion.22
  13.9 1.3 fusion.29
  18.0 12.3 %all-reduce.8 = (f32[8]{0:T(128)S(1)}, f32[8]{0:T(128)S(1)}) all-reduce(f32[8]{0:T(128)S(1)} %dynamic-update-slice, f32[8]{0:T(128)S(1)} %dynamic-update-slice.1), channel_id=1, replica_groups=mesh['outer'=32,'inner'=8] {'inner'}, use_global_device_ids=true, to_apply=%add.2 | all-reduce | flops 16 | bytes 128
  30.2 20.8 %all-gather.6.cloned.1.call-done = f32[80,144,64]{1,2,0:T(8,128)} async-done(((f32[10,144,64]{1,2,0:T(8,128)}), f32[80,144,64]{1,2,0:T(8,128)}) %all-gather.6.cloned.1.call-update) | async-done | bytes 2949136 | tf_op jit(solution)/shard_map/all_gather | solution.py:19
  51.1 38.8 %while.39 = (s32[]{:T(128)}, f32[10,144,64]{2,1,0:T(8,128)S(1)}, f32[]{:T(128)}, f32[]{:T(128)}, s32[]{:T(128)}, /*index=5*/f32[8]{0:T(128)S(1)}, f32[8,10,144,6...) while((s32[]{:T(128)}, f32[10,144,64]{2,1,0:T(8,128)S(1)}, ...), condition=%wide.region_2.3_spmd, body=%wide.region_1.2_spmd.sunk | while | flops 276490 | bytes 2580718 | solution.py:27
  91.4 65.7 %all-reduce.11.cloned.1.call-done = f32[1,10,144,64]{2,3,1,0:T(8,128)} async-done(((f32[1,10,144,64]{2,3,1,0:T(8,128)}), f32[1,10,144,64]{2,3,1,0:T(8,128)}) %all-reduce.11.cloned.1.call-update) | async-done | bytes 368656 | tf_op jit(solution)/shard_map/psum | solution.py:32
  157.1 1.3 collective-permute-start
  158.4 1.3 collective-permute-start.1
  159.7 1.3 collective-permute-start.2
  161.0 1.3 collective-permute-start.3
  162.3 1.3 collective-permute-start.4
  164.9 2.0 fusion.17
  166.9 1.9 collective-permute-done
  168.8 1.3 collective-permute-start.5
  170.0 1.7 constant_dynamic-update-slice_fusion.9
  171.8 2.5 collective-permute-done.1
  174.3 1.3 collective-permute-start.6
  175.6 1.7 constant_dynamic-update-slice_fusion.8
  177.3 1.3 collective-permute-start.7
  179.4 3.3 collective-permute-done.3
  182.7 1.3 collective-permute-start.8
  184.7 4.2 collective-permute-done.4
  188.9 1.3 collective-permute-start.9
  190.9 6.0 collective-permute-done.5
  196.9 1.3 collective-permute-start.10
  198.9 1.3 collective-permute-start.11
  201.0 1.3 collective-permute-start.12
  203.8 23.1 %collective-permute-done.8 = bf16[128,1280]{1,0:T(8,128)(2,1)S(1)} collective-permute-done((bf16[128,1280]{1,0:T(8,128)(2,1)S(1)}, bf16[128,1280]{1,0:T(8,128)(2,1)S(1)}, u32[]{:S(2)}, u32[]{:S(2)}) %collective-permute-start.8) | collective-permute-done | bytes 327712 | tf_op jit(solution)/shard_map/ppermute | solution.py:38
  226.9 1.3 collective-permute-start.13
  229.0 10.2 %collective-permute-done.9 = bf16[128,1280]{1,0:T(8,128)(2,1)S(1)} collective-permute-done((bf16[128,1280]{1,0:T(8,128)(2,1)S(1)}, bf16[128,1280]{1,0:T(8,128)(2,1)S(1)}, u32[]{:S(2)}, u32[]{:S(2)}) %collective-permute-start.9) | collective-permute-done | bytes 327712 | tf_op jit(solution)/shard_map/ppermute | solution.py:38
  239.1 1.3 collective-permute-start.14
  241.2 1.3 collective-permute-start.15
  244.8 6.3 %collective-permute-done.13 = bf16[128,1280]{1,0:T(8,128)(2,1)S(1)} collective-permute-done((bf16[128,1280]{1,0:T(8,128)(2,1)S(1)}, bf16[128,1280]{1,0:T(8,128)(2,1)S(1)}, u32[]{:S(2)}, u32[]{:S(2)}) %collective-permute-start.13) | collective-permute-done | bytes 327712 | tf_op jit(solution)/shard_map/ppermute | solution.py:38
  251.9 9.7 %collective-permute-done.14 = bf16[128,1280]{1,0:T(8,128)(2,1)S(1)} collective-permute-done((bf16[128,1280]{1,0:T(8,128)(2,1)S(1)}, bf16[128,1280]{1,0:T(8,128)(2,1)S(1)}, u32[]{:S(2)}, u32[]{:S(2)}) %collective-permute-start.14) | collective-permute-done | bytes 327712 | tf_op jit(solution)/shard_map/ppermute | solution.py:38
  263.9 31.7 %all-reduce.7 = (f32[1]{0:T(128)}, f32[1]{0:T(128)}) all-reduce(f32[1]{0:T(128)} %bitcast.14, f32[1]{0:T(128)} %bitcast.17), channel_id=1, replica_groups=mesh['outer'=32,'inner'=8] {'inner'}, use_global_device_ids=true, to_apply=%region_4.5 | all-reduce | flops 2 | bytes 16 | tf_op jit(solution)/shard_map/psum | solution.py:32
  295.6 1.4 dynamic-update-slice.3
  296.9 1.3 dynamic-update-slice.2
  298.2 81.5 %all-reduce.6 = (f32[32]{0:T(128)S(1)}, f32[32]{0:T(128)S(1)}) all-reduce(f32[32]{0:T(128)S(1)} %dynamic-update-slice.2, f32[32]{0:T(128)S(1)} %dynamic-update-slice.3), channel_id=1, replica_groups=mesh['outer'=32,'inner'=8] {'outer'}, use_global_device_ids=true, to_apply=%add.4 | all-reduce | flops 64 | bytes 512
  379.7 17.1 %all-gather.4.cloned.1.call-done = f32[32,10,144,64]{2,3,1,0:T(8,128)} async-done(((f32[1,10,144,64]{2,3,1,0:T(8,128)}), f32[32,10,144,64]{2,3,1,0:T(8,128)}) %all-gather.4.cloned.1.call-update) | async-done | bytes 11796496 | tf_op jit(solution)/shard_map/all_gather | solution.py:19
  396.9 167.7 %while.40 = (s32[]{:T(128)}, f32[10,144,64]{2,1,0:T(8,128)S(1)}, f32[]{:T(128)}, f32[]{:T(128)}, s32[]{:T(128)}, /*index=5*/f32[32]{0:T(128)S(1)}, f32[32,10,144...) while((s32[]{:T(128)}, f32[10,144,64]{2,1,0:T(8,128)S(1)}, ...), condition=%wide.region_7.8_spmd, body=%wide.region_6.7_spmd.sunk | while | flops 276490 | bytes 2580718 | solution.py:27
  564.6 48.9 %while.41 = (s32[]{:T(128)}, bf16[10,128,128]{1,2,0:T(8,128)(2,1)}, s32[10]{0:T(128)S(1)}, bf16[128,1280]{1,0:T(8,128)(2,1)}, bf16[1152,1280]{1,0:T(8,128)(2,1)}...) while((s32[]{:T(128)}, bf16[10,128,128]{1,2,0:T(8,128)(2,1)}, ...), condition=%wide.region_13.14_spmd.clone, body=%wide.region_10.13_spmd.clone.sunk | while | flops 77299456 | bytes 2566339 | solution.py:150
  565.9 1.4 fusion.50
  567.5 1.3 fusion.52
  570.8 1.4 fusion.50
  572.4 1.3 fusion.52
  575.7 1.4 fusion.50
  577.3 1.3 fusion.52
  580.6 1.4 fusion.50
  582.2 1.3 fusion.52
  585.4 1.4 fusion.50
  587.1 1.3 fusion.52
  590.3 1.4 fusion.50
  592.0 1.3 fusion.52
  595.2 1.4 fusion.50
  596.9 1.3 fusion.52
  600.1 1.4 fusion.50
  601.8 1.3 fusion.52
  605.0 1.4 fusion.50
  606.6 1.3 fusion.52
  609.9 1.4 fusion.50
  611.5 1.3 fusion.52
  613.6 1.9 copy.48
  (315 shorter events, 148.0 us)
Async XLA Ops:
  7.2 8.7 %copy-start.8 = (u32[256]{0:T(256)S(1)}, u32[256]{0:T(256)}, u32[]{:S(2)}) copy-start(u32[256]{0:T(256)} %constant.106) | copy-start | bytes 3076
  7.2 6.7 %copy-start.5 = (s32[128]{0:T(128)S(1)}, s32[128]{0:T(128)}, u32[]{:S(2)}) copy-start(s32[128]{0:T(128)} %param.18) | copy-start | bytes 1540
  7.2 43.9 %all-gather.6.cloned.1.call-start = ((), (), s32[]{:S(2)}) async-start(), calls=%async_computation.2 | async-start | bytes 5898240 | tf_op jit(solution)/shard_map/all_gather | solution.py:19
  13.2 143.9 %all-reduce.11.cloned.1.call-start = ((), (), s32[]{:S(2)}) async-start(), calls=%async_computation | async-start | bytes 1310720 | tf_op jit(solution)/shard_map/psum | solution.py:32
  51.1 39.2 %copy-start = (f32[10,144,64]{1,2,0:T(8,128)S(1)}, f32[10,144,64]{1,2,0:T(8,128)}, u32[]{:S(2)}) copy-start(f32[10,144,64]{1,2,0:T(8,128)} %fusion.22) | copy-start | bytes 1105924
  89.9 67.2 %copy-start.1 = (bf16[128,1280]{1,0:T(8,128)(2,1)S(1)}, bf16[128,1280]{1,0:T(8,128)(2,1)}, u32[]{:S(2)}) copy-start(bf16[128,1280]{1,0:T(8,128)(2,1)} %param.20) | copy-start | bytes 983044
  89.9 73.7 %copy-start.7 = (u32[256]{0:T(256)S(1)}, u32[256]{0:T(256)}, u32[]{:S(2)}) copy-start(u32[256]{0:T(256)} %constant.116) | copy-start | bytes 3076
  89.9 74.4 %copy-start.4 = (bf16[128,110]{0,1:T(8,128)(2,1)S(1)}, bf16[128,110]{0,1:T(8,128)(2,1)}, u32[]{:S(2)}) copy-start(bf16[128,110]{0,1:T(8,128)(2,1)} %param.14) | copy-start | bytes 84484
  90.3 74.2 %copy-start.6 = (f32[640]{0:T(1024)S(1)}, f32[640]{0:T(1024)}, u32[]{:S(2)}) copy-start(f32[640]{0:T(1024)} %param.17) | copy-start | bytes 7684
  91.3 91.4 %copy-start.2 = (bf16[128,1280]{1,0:T(8,128)(2,1)S(1)}, bf16[128,1280]{1,0:T(8,128)(2,1)}, u32[]{:S(2)}) copy-start(bf16[128,1280]{1,0:T(8,128)(2,1)} %param.21) | copy-start | bytes 983044
  91.3 305.5 %all-gather.4.cloned.1.call-start = ((), (), s32[]{:S(2)}) async-start(), calls=%async_computation.1 | async-start | bytes 21626880 | tf_op jit(solution)/shard_map/all_gather | solution.py:19
  157.1 11.6 %collective-permute-start = (bf16[128,1280]{1,0:T(8,128)(2,1)S(1)}, bf16[128,1280]{1,0:T(8,128)(2,1)}, u32[]{:S(2)}, u32[]{:S(2)}) collective-permute-start(bf16[128,1280]{1,0:T(8,128)(2,1)S(1)} %copy-done.1), channel_id=1, source_target_pairs={{0,8},{1,9},{2,10},{3,11},{4,12},{5,13},{6,14},{7,15},{8,16},{9,17... | collective-permute-start | bytes 983048 | tf_op jit(solution)/shard_map/ppermute | solution.py:38
  158.4 15.9 %collective-permute-start.1 = (bf16[128,1280]{1,0:T(8,128)(2,1)S(1)}, bf16[128,1280]{1,0:T(8,128)(2,1)}, u32[]{:S(2)}, u32[]{:S(2)}) collective-permute-start(bf16[128,1280]{1,0:T(8,128)(2,1)S(1)} %copy-done.1), channel_id=1, source_target_pairs={{0,7},{1,8},{2,9},{3,10},{4,11},{5,12},{6,13},{7,14},{8,15},{9,16}... | collective-permute-start | bytes 983048 | tf_op jit(solution)/shard_map/ppermute | solution.py:38
  159.7 17.6 %collective-permute-start.2 = (bf16[128,1280]{1,0:T(8,128)(2,1)S(1)}, bf16[128,1280]{1,0:T(8,128)(2,1)S(1)}, u32[]{:S(2)}, u32[]{:S(2)}) collective-permute-start(bf16[128,1280]{1,0:T(8,128)(2,1)S(1)} %copy-done.1), channel_id=1, source_target_pairs={{0,6},{1,7},{2,8},{3,9},{4,10},{5,11},{6,12},{7,13},{8,14},{9,15},... | collective-permute-start | bytes 983048 | tf_op jit(solution)/shard_map/ppermute | solution.py:38
  161.0 21.7 %collective-permute-start.3 = (bf16[128,1280]{1,0:T(8,128)(2,1)S(1)}, bf16[128,1280]{1,0:T(8,128)(2,1)S(1)}, u32[]{:S(2)}, u32[]{:S(2)}) collective-permute-start(bf16[128,1280]{1,0:T(8,128)(2,1)S(1)} %copy-done.1), channel_id=1, source_target_pairs={{0,5},{1,6},{2,7},{3,8},{4,9},{5,10},{6,11},{7,12},{8,13},{9,14},{... | collective-permute-start | bytes 983048 | tf_op jit(solution)/shard_map/ppermute | solution.py:38
  162.3 26.6 %collective-permute-start.4 = (bf16[128,1280]{1,0:T(8,128)(2,1)S(1)}, bf16[128,1280]{1,0:T(8,128)(2,1)S(1)}, u32[]{:S(2)}, u32[]{:S(2)}) collective-permute-start(bf16[128,1280]{1,0:T(8,128)(2,1)S(1)} %copy-done.1), channel_id=1, source_target_pairs={{0,4},{1,5},{2,6},{3,7},{4,8},{5,9},{6,10},{7,11},{8,12},{9,13},{1... | collective-permute-start | bytes 983048 | tf_op jit(solution)/shard_map/ppermute | solution.py:38
  168.8 28.1 %collective-permute-start.5 = (bf16[128,1280]{1,0:T(8,128)(2,1)S(1)}, bf16[128,1280]{1,0:T(8,128)(2,1)S(1)}, u32[]{:S(2)}, u32[]{:S(2)}) collective-permute-start(bf16[128,1280]{1,0:T(8,128)(2,1)S(1)} %copy-done.1), channel_id=1, source_target_pairs={{0,3},{1,4},{2,5},{3,6},{4,7},{5,8},{6,9},{7,10},{8,11},{9,12},{10... | collective-permute-start | bytes 983048 | tf_op jit(solution)/shard_map/ppermute | solution.py:38
  174.3 24.6 %collective-permute-start.6 = (bf16[128,1280]{1,0:T(8,128)(2,1)S(1)}, bf16[128,1280]{1,0:T(8,128)(2,1)S(1)}, u32[]{:S(2)}, u32[]{:S(2)}) collective-permute-start(bf16[128,1280]{1,0:T(8,128)(2,1)S(1)} %copy-done.1), channel_id=1, source_target_pairs={{0,2},{1,3},{2,4},{3,5},{4,6},{5,7},{6,8},{7,9},{8,10},{9,11},{10,... | collective-permute-start | bytes 983048 | tf_op jit(solution)/shard_map/ppermute | solution.py:38
  177.3 23.6 %collective-permute-start.7 = (bf16[128,1280]{1,0:T(8,128)(2,1)S(1)}, bf16[128,1280]{1,0:T(8,128)(2,1)S(1)}, u32[]{:S(2)}, u32[]{:S(2)}) collective-permute-start(bf16[128,1280]{1,0:T(8,128)(2,1)S(1)} %copy-done.1), channel_id=1, source_target_pairs={{0,1},{1,2},{2,3},{3,4},{4,5},{5,6},{6,7},{7,8},{8,9},{9,10},{10,1... | collective-permute-start | bytes 983048 | tf_op jit(solution)/shard_map/ppermute | solution.py:38
  182.7 44.2 %collective-permute-start.8 = (bf16[128,1280]{1,0:T(8,128)(2,1)S(1)}, bf16[128,1280]{1,0:T(8,128)(2,1)S(1)}, u32[]{:S(2)}, u32[]{:S(2)}) collective-permute-start(bf16[128,1280]{1,0:T(8,128)(2,1)S(1)} %copy-done.2), channel_id=1, source_target_pairs={{0,8},{1,9},{2,10},{3,11},{4,12},{5,13},{6,14},{7,15},{8,16},{9,17... | collective-permute-start | bytes 983048 | tf_op jit(solution)/shard_map/ppermute | solution.py:38
  188.9 50.2 %collective-permute-start.9 = (bf16[128,1280]{1,0:T(8,128)(2,1)S(1)}, bf16[128,1280]{1,0:T(8,128)(2,1)S(1)}, u32[]{:S(2)}, u32[]{:S(2)}) collective-permute-start(bf16[128,1280]{1,0:T(8,128)(2,1)S(1)} %copy-done.2), channel_id=1, source_target_pairs={{0,7},{1,8},{2,9},{3,10},{4,11},{5,12},{6,13},{7,14},{8,15},{9,16}... | collective-permute-start | bytes 983048 | tf_op jit(solution)/shard_map/ppermute | solution.py:38
  196.9 44.3 %collective-permute-start.10 = (bf16[128,1280]{1,0:T(8,128)(2,1)S(1)}, bf16[128,1280]{1,0:T(8,128)(2,1)S(1)}, u32[]{:S(2)}, u32[]{:S(2)}) collective-permute-start(bf16[128,1280]{1,0:T(8,128)(2,1)S(1)} %copy-done.2), channel_id=1, source_target_pairs={{0,6},{1,7},{2,8},{3,9},{4,10},{5,11},{6,12},{7,13},{8,14},{9,15},... | collective-permute-start | bytes 983048 | tf_op jit(solution)/shard_map/ppermute | solution.py:38
  198.9 44.3 %collective-permute-start.11 = (bf16[128,1280]{1,0:T(8,128)(2,1)S(1)}, bf16[128,1280]{1,0:T(8,128)(2,1)S(1)}, u32[]{:S(2)}, u32[]{:S(2)}) collective-permute-start(bf16[128,1280]{1,0:T(8,128)(2,1)S(1)} %copy-done.2), channel_id=1, source_target_pairs={{0,5},{1,6},{2,7},{3,8},{4,9},{5,10},{6,11},{7,12},{8,13},{9,14},{... | collective-permute-start | bytes 983048 | tf_op jit(solution)/shard_map/ppermute | solution.py:38
  201.0 43.1 %collective-permute-start.12 = (bf16[128,1280]{1,0:T(8,128)(2,1)S(1)}, bf16[128,1280]{1,0:T(8,128)(2,1)S(1)}, u32[]{:S(2)}, u32[]{:S(2)}) collective-permute-start(bf16[128,1280]{1,0:T(8,128)(2,1)S(1)} %copy-done.2), channel_id=1, source_target_pairs={{0,4},{1,5},{2,6},{3,7},{4,8},{5,9},{6,10},{7,11},{8,12},{9,13},{1... | collective-permute-start | bytes 983048 | tf_op jit(solution)/shard_map/ppermute | solution.py:38
  226.9 24.2 %collective-permute-start.13 = (bf16[128,1280]{1,0:T(8,128)(2,1)S(1)}, bf16[128,1280]{1,0:T(8,128)(2,1)S(1)}, u32[]{:S(2)}, u32[]{:S(2)}) collective-permute-start(bf16[128,1280]{1,0:T(8,128)(2,1)S(1)} %copy-done.2), channel_id=1, source_target_pairs={{0,3},{1,4},{2,5},{3,6},{4,7},{5,8},{6,9},{7,10},{8,11},{9,12},{10... | collective-permute-start | bytes 983048 | tf_op jit(solution)/shard_map/ppermute | solution.py:38
  239.1 22.5 %collective-permute-start.14 = (bf16[128,1280]{1,0:T(8,128)(2,1)S(1)}, bf16[128,1280]{1,0:T(8,128)(2,1)S(1)}, u32[]{:S(2)}, u32[]{:S(2)}) collective-permute-start(bf16[128,1280]{1,0:T(8,128)(2,1)S(1)} %copy-done.2), channel_id=1, source_target_pairs={{0,2},{1,3},{2,4},{3,5},{4,6},{5,7},{6,8},{7,9},{8,10},{9,11},{10,... | collective-permute-start | bytes 983048 | tf_op jit(solution)/shard_map/ppermute | solution.py:38
  241.2 21.2 %collective-permute-start.15 = (bf16[128,1280]{1,0:T(8,128)(2,1)S(1)}, bf16[128,1280]{1,0:T(8,128)(2,1)S(1)}, u32[]{:S(2)}, u32[]{:S(2)}) collective-permute-start(bf16[128,1280]{1,0:T(8,128)(2,1)S(1)} %copy-done.2), channel_id=1, source_target_pairs={{0,1},{1,2},{2,3},{3,4},{4,5},{5,6},{6,7},{7,8},{8,9},{9,10},{10,1... | collective-permute-start | bytes 983048 | tf_op jit(solution)/shard_map/ppermute | solution.py:38
  613.6 2.8 copy-start.3
Sparse Core Ops, SparseCore 0:
  13.3 37.7 all-gather.5
  91.5 65.5 all-reduce.10
  159.7 237.0 all-gather.3
where the time goes:
time: 629 us; the launch traced here: 624 us
  waiting for transfers between devices  171 us (27%)
  local copies, waits for them, and re-layouts  143 us (23%)
  blocking collectives  125 us (20%)
  loops' own time  102 us (16%)
  matrix products  30.6 us (5%)
  starting transfers between devices  20.7 us (3%)
  between operations  15.5 us (2%)
  other arithmetic  15.4 us (2%)
    dynamic_slice x152, local copies, waits for them, and re-layouts, one(): lax.dynamic_index_in_dim(a, step, 0, False)  103 us
    another operation x2, loops' own time, entering(): return lax.fori_loop(0, place, one, state)  95.5 us
    unnamed x2, blocking collectives  93.8 us
    ppermute x16, waiting for transfers between devices, shifted(): return lax.ppermute(block, axis, route)  67.2 us
    psum x1, waiting for transfers between devices, broadcast(): return lax.psum(block, axis)  65.7 us
    all_gather x2, waiting for transfers between devices, entering(): gathered = jax.tree.map(lambda a: lax.all_gather(a, axis), part)  37.9 us
    psum x1, blocking collectives, broadcast(): return lax.psum(block, axis)  31.7 us
    unnamed x46, local copies, waits for them, and re-layouts  22.5 us
  transfers between devices with their start and end apart: 19, of which 12 were waited for; matrix products, arithmetic and copies ran while one was open for 4% of the time, Pallas kernels for 0%

commit v1 on v0

v1 whole, which is shorter than its diff:
```python
import functools
import math

import jax
import jax.numpy as jnp
import numpy as np
from jax import lax
from jax.experimental import pallas as pl
from jax.experimental.pallas import tpu as pltpu
from jax.sharding import PartitionSpec as P

HEADS = 10
BASED_DIM = 64
HEAD_DIM = 128
QK_DIM = 11
WIN_HEADS = 10
ROWS = 128
BACK = 8
FEAT = 80
PAIRS = HEADS // 2
SLICE = 64
MESH = pl.DeviceIdType.MESH
ORDER = ((0, 1), (1, 0), (1, 1), (3, 0), (3, 1), (2, 0), (2, 1))
NT = (((1,), (1,)), ((), ()))
TN = (((0,), (0,)), ((), ()))
F32 = jnp.float32
BF16 = jnp.bfloat16


def feature_table():
    table = np.zeros((8, HEADS * 128), np.float32)
    table[:2] = -1.0
    for head in range(HEADS):
        at = head * 128
        for a in range(QK_DIM + 1):
            for b in range(a, QK_DIM + 1):
                for row, entry in ((0, a), (1, b)):
                    if entry == 0:
                        table[row + 2, at] = 1.0
                    else:
                        table[row, at] = head * QK_DIM + entry - 1
                table[4, at] = 1.0 if a == b else 2.0
                at += 1
    return table


def kernel(
    outer,
    bq, bk, bv, gain, doc, aux, wq, wk, wv,
    bout, wout,
    kv, cfw, qb, ob, dsl, dk, d2, ssend, srecv, tsend, trecv, fsend, pf, tot, phq,
    rs_own, ss_own, rs_prev, ss_prev, rs_q, ss_q, rs_o, ss_o, rs_c, ss_c,
    rs_d, ss_d, rs_dk, ss_dk, rs_s, ss_s, rs_t, ss_t, rs_f, ss_f,
):
    r = lax.axis_index("outer")
    i = lax.axis_index("inner")
    x = i // 2
    c = i % 2
    up = lax.rem(r + 1, outer)

    def to(dx, dc):
        return lax.rem(x + dx, 4) * 2 + lax.rem(c + dc, 2)

    def frm(dx, dc):
        return lax.rem(x + 4 - dx, 4) * 2 + lax.rem(c + dc, 2)

    def cols(ref, head):
        return ref.at[:, pl.ds(pl.multiple_of(head * HEAD_DIM, HEAD_DIM), HEAD_DIM)]

    def remote(src, dst, ss, rs, row, inner):
        return pltpu.make_async_remote_copy(
            src_ref=src, dst_ref=dst, send_sem=ss, recv_sem=rs,
            device_id=(row, inner), device_id_type=MESH,
        )

    def arrived(dst, rs):
        pltpu.make_async_copy(dst, dst, rs).wait()

    sent = []

    def send(src, dst, ss, rs, row, inner):
        copy = remote(src, dst, ss, rs, row, inner)
        copy.start()
        sent.append((src, ss))

    doc_row = doc[...].astype(F32)
    dsl[i] = jnp.broadcast_to(doc_row, (8, 128))

    barrier = pltpu.get_barrier_semaphore()
    for dx, dc in ORDER:
        pl.semaphore_signal(barrier, inc=1, device_id=(r, to(dx, dc)), device_id_type=MESH)
    for k in range(1, BACK + 1):
        pl.semaphore_signal(
            barrier, inc=1, device_id=(lax.rem(r + outer - k, outer), i), device_id_type=MESH
        )
    pl.semaphore_wait(barrier, len(ORDER) + BACK)

    for h in range(2):
        for part, ref in ((0, wk), (1, wv)):
            send(cols(ref, 8 + h), cfw.at[h, part], ss_c.at[h, part], rs_c.at[h, part], up, i)
    for part, ref in ((0, wk), (1, wv)):
        pltpu.make_async_copy(cols(ref, i), kv.at[0, 8 + i, part], rs_own.at[0, i, part]).start()
        pltpu.make_async_copy(cols(ref, 8 + c), kv.at[1, 8 + i, part], rs_own.at[1, i, part]).start()
    pltpu.make_async_copy(cols(wq, i), qb.at[i], rs_q.at[i]).start()
    pltpu.make_async_copy(cols(wq, 8 + c), qb.at[8 + c], rs_q.at[8 + c]).start()
    for n, (dx, dc) in enumerate(ORDER):
        d = to(dx, dc)
        send(dsl.at[i], dsl.at[i], ss_d.at[n], rs_d.at[i], r, d)
    for n, (dx, dc) in enumerate(ORDER):
        d = to(dx, dc)
        for part, ref in ((0, wk), (1, wv)):
            send(
                cols(ref, d), kv.at[0, 8 + i, part], ss_own.at[0, n, part],
                rs_own.at[0, i, part], r, d,
            )
    sib = x * 2 + (1 - c)
    for part, ref in ((0, wk), (1, wv)):
        send(
            cols(ref, 9 - c), kv.at[1, 8 + i, part], ss_own.at[1, 0, part],
            rs_own.at[1, i, part], r, sib,
        )
    send(cols(wq, 9 - c), qb.at[8 + c], ss_q.at[7], rs_q.at[8 + c], r, sib)

    for part in range(2):
        arrived(kv.at[0, 8 + i, part], rs_own.at[0, i, part])
    send(kv.at[0, 8 + i], kv.at[0, i], ss_prev.at[0, i], rs_prev.at[0, i], up, i)

    table = aux[...]
    lane110 = lax.broadcasted_iota(jnp.int32, (QK_DIM * HEADS, HEADS * 128), 0).astype(F32)
    pick_a = jnp.where(lane110 == table[0:1, :], 0.5, 0.0).astype(BF16)
    pick_b = jnp.where(lane110 == table[1:2, :], 0.5, 0.0).astype(BF16)
    xq = bq[...]
    xk = bk[...]

    def features(proj):
        first = jnp.dot(proj, pick_a, preferred_element_type=F32) + table[2:3, :]
        second = jnp.dot(proj, pick_b, preferred_element_type=F32) + table[3:4, :]
        return first * second

    lane = lax.broadcasted_iota(jnp.int32, (128, 128), 1)
    row = lax.broadcasted_iota(jnp.int32, (128, 128), 0)
    own_rows = jnp.broadcast_to(doc_row, (128, 128))
    own_cols = own_rows.T
    keep = own_cols == doc_row[:, 127:128]
    fk = features(xk).astype(BF16)
    left80 = lax.broadcasted_iota(jnp.int32, (128, 128), 1) < BASED_DIM
    for p in range(PAIRS):
        vals = bv[:, p * 128 : (p + 1) * 128]
        kept = jnp.where(keep, vals.astype(F32), 0.0).astype(BF16)
        both = [
            lax.dot_general(
                fk[:, h * 128 : (h + 1) * 128], kept, TN, preferred_element_type=F32
            )
            for h in (2 * p, 2 * p + 1)
        ]
        state = jnp.where(left80, both[0], both[1])
        ssend[p * FEAT : (p + 1) * FEAT, :] = state[:FEAT].astype(BF16)
    ssend[PAIRS * FEAT :, :] = jnp.zeros((8 * SLICE - PAIRS * FEAT, 128), BF16)

    def block(ref, d):
        return ref.at[pl.ds(pl.multiple_of(d * SLICE, SLICE), SLICE)]

    pltpu.make_async_copy(block(ssend, i), srecv.at[i], rs_s.at[i]).start()
    for n, (dx, dc) in enumerate(ORDER):
        d = to(dx, dc)
        send(block(ssend, d), srecv.at[i], ss_s.at[n], rs_s.at[i], r, d)

    for h in range(2):
        for part in range(2):
            arrived(cfw.at[h, part], rs_c.at[h, part])
    pltpu.make_async_copy(cfw.at[c], kv.at[1, i], rs_prev.at[1, i]).start()
    send(cfw.at[1 - c], kv.at[1, i], ss_prev.at[1, 0], rs_prev.at[1, i], r, sib)
    for dx in (1, 3, 2):
        for dc in range(2):
            n = dx * 2 + dc - 1
            h = lax.rem(c + dc, 2)
            d = to(dx, dc)

            @pl.when(x + dx < 4)
            def _():
                for part, ref in ((0, wk), (1, wv)):
                    remote(
                        cols(ref, 8 + h), kv.at[1, 8 + i, part], ss_own.at[1, n, part],
                        rs_own.at[1, i, part], r, d,
                    ).start()

            @pl.when(x + dx >= 4)
            def _():
                remote(
                    cfw.at[h], kv.at[1, i], ss_prev.at[1, n], rs_prev.at[1, i], r, d
                ).start()

    for n, (dx, dc) in enumerate(ORDER):
        s = frm(dx, dc)
        for part in range(2):
            arrived(kv.at[0, 8 + s, part], rs_own.at[0, s, part])
        send(kv.at[0, 8 + s], kv.at[0, s], ss_prev.at[0, s], rs_prev.at[0, s], up, i)
    for n, (dx, dc) in enumerate(ORDER):
        d = to(dx, dc)
        send(cols(wq, d), qb.at[i], ss_q.at[n], rs_q.at[i], r, d)

    for dx, dc in ORDER:
        s = frm(dx, dc)
        arrived(dsl.at[s], rs_d.at[s])
    sub = lax.broadcasted_iota(jnp.int32, (8, 128), 0)
    row_docs = jnp.zeros((8, 128), F32)
    for s in range(8):
        row_docs = jnp.where(sub == s, dsl[s], row_docs)
    dk[0] = row_docs
    for k in range(1, BACK + 1):
        send(dk.at[0], dk.at[k], ss_dk.at[k], rs_dk.at[k], lax.rem(r + k, outer), i)

    arrived(srecv.at[i], rs_s.at[i])
    for dx, dc in ORDER:
        s = frm(dx, dc)
        arrived(srecv.at[s], rs_s.at[s])
    last = [row_docs[s : s + 1, 127:128] for s in range(8)]
    acc = srecv[0].astype(F32)
    running = []
    for s in range(1, 8):
        running.append(acc)
        acc = srecv[s].astype(F32) + jnp.where(last[s] == last[s - 1], acc, 0.0)
    tsend[...] = acc
    for k in range(1, BACK + 1):
        send(tsend, trecv.at[k - 1], ss_t.at[k], rs_t.at[k], lax.rem(r + k, outer), i)

    inside = (own_cols == own_rows) & (lane <= row)
    lane_q = lax.broadcasted_iota(jnp.int32, (128, QK_DIM * HEADS), 1)
    for p in range(PAIRS):
        vals = bv[:, p * 128 : (p + 1) * 128]
        both = []
        for h in (2 * p, 2 * p + 1):
            mine = (lane_q >= h * QK_DIM) & (lane_q < (h + 1) * QK_DIM)
            part_q = jnp.where(mine, xq.astype(F32), 0.0).astype(BF16)
            dots = lax.dot_general(part_q, xk, NT, preferred_element_type=F32) * 0.25 + 1.0
            weight = jnp.where(inside, dots * dots, 0.0).astype(BF16)
            both.append(jnp.dot(weight, vals, preferred_element_type=F32))
        tot[p] = jnp.where(left80, both[0], both[1])
    phq[...] = (features(xq) * table[4:5, :]).astype(BF16)

    for k in range(1, BACK + 1):
        arrived(dk.at[k], rs_dk.at[k])
        arrived(trecv.at[k - 1], rs_t.at[k])
    entering_doc = jnp.where(r >= 1, dk[1][7:8, 127:128], -1.0)
    enter = jnp.zeros((SLICE, 128), F32)
    for k in range(1, BACK + 1):
        same = jnp.where(r >= k, dk[k][7:8, 127:128], -2.0) == entering_doc
        enter = enter + jnp.where(same, trecv[k - 1], 0.0)
    fsend[0] = enter.astype(BF16)
    for s in range(1, 8):
        fsend[s] = (running[s - 1] + jnp.where(last[s - 1] == entering_doc, enter, 0.0)).astype(BF16)
    pltpu.make_async_copy(fsend.at[i], block(pf, i), rs_f.at[i]).start()
    for n, (dx, dc) in enumerate(ORDER):
        d = to(dx, dc)
        send(fsend.at[d], block(pf, i), ss_f.at[n], rs_f.at[i], r, d)
    d2[0:8] = jnp.where(r >= 1, dk[1], -1.0)
    d2[8:16] = row_docs

    factor = math.log2(math.e) / math.sqrt(HEAD_DIM)

    def attend(b, j, at):
        query = qb[at]
        docq = jnp.broadcast_to(d2[pl.ds(8 + j, 1), :], (128, 128)).T
        scores = []
        top = None
        for t in range(BACK + 1):
            block_scores = lax.dot_general(
                query, kv[b, j + t, 0], NT, preferred_element_type=F32
            )
            see = docq == d2[pl.ds(j + t, 1), :]
            if t == 0:
                see = see & (lane > row)
            if t == BACK:
                see = see & (lane <= row)
            block_scores = jnp.where(see, block_scores, -1e30)
            scores.append(block_scores)
            top = block_scores if top is None else jnp.maximum(top, block_scores)
        peak = jnp.max(top, axis=1, keepdims=True)
        whole = None
        mixed = None
        for t in range(BACK + 1):
            prob = jnp.exp2((scores[t] - peak) * factor)
            whole = prob if whole is None else whole + prob
            term = jnp.dot(prob.astype(BF16), kv[b, j + t, 1], preferred_element_type=F32)
            mixed = term if mixed is None else mixed + term
        rowsum = jnp.sum(whole, axis=1, keepdims=True)
        ob[at] = (mixed / rowsum).astype(BF16)

    arrived(qb.at[8 + c], rs_q.at[8 + c])
    arrived(qb.at[9 - c], rs_q.at[9 - c])

    @pl.loop(0, 2 * x + 2)
    def _(s):
        for part in range(2):
            arrived(kv.at[1, 8 + s, part], rs_own.at[1, s, part])

    @pl.loop(2 * x, 8)
    def _(s):
        arrived(kv.at[1, s], rs_prev.at[1, s])

    @pl.loop(0, 2)
    def _(core):
        attend(1, 2 * x + core, 8 + core)

    send(ob.at[9 - c], cols(wout, 8 + c), ss_o.at[8], rs_o.at[8 + c], r, sib)
    pltpu.make_async_copy(ob.at[8 + c], cols(wout, 8 + c), ss_o.at[9]).start()

    @pl.loop(0, 8)
    def _(step):
        j = 7 - step

        arrived(qb.at[j], rs_q.at[j])
        arrived(kv.at[0, j], rs_prev.at[0, j])
        attend(0, j, j)

        @pl.when(j != i)
        def _():
            remote(ob.at[j], cols(wout, i), ss_o.at[j], rs_o.at[i], r, j).start()

        @pl.when(j == i)
        def _():
            pltpu.make_async_copy(ob.at[j], cols(wout, i), ss_o.at[j]).start()

    arrived(block(pf, i), rs_f.at[i])
    for dx, dc in ORDER:
        s = frm(dx, dc)
        arrived(block(pf, s), rs_f.at[s])
    previous = jnp.where(i == 0, entering_doc, -1.0)
    for s in range(1, 8):
        previous = jnp.where(i == s, last[s - 1], previous)
    carried = own_cols == previous
    rest = jnp.zeros((128 - FEAT, 128), BF16)
    for p in range(PAIRS):
        state = jnp.concatenate([pf[p * FEAT : (p + 1) * FEAT, :], rest], axis=0)
        both = [
            jnp.dot(phq[:, h * 128 : (h + 1) * 128], state, preferred_element_type=F32)
            for h in (2 * p, 2 * p + 1)
        ]
        total = tot[p] + jnp.where(carried, jnp.where(left80, both[0], both[1]), 0.0)
        square = total * total
        one = jnp.sum(jnp.where(left80, square, 0.0), axis=1, keepdims=True)
        two = jnp.sum(jnp.where(left80, 0.0, square), axis=1, keepdims=True)
        mean = jnp.where(left80, one, two) * (1.0 / BASED_DIM)
        scaled = total * lax.rsqrt(mean + 1e-5) * gain[:, p * 128 : (p + 1) * 128]
        bout[:, p * 128 : (p + 1) * 128] = scaled.astype(BF16)

    @pl.loop(0, 8)
    def _(j):
        @pl.when(j != i)
        def _():
            arrived(cols(wout, j), rs_o.at[j])

    arrived(cols(wout, 9 - c), rs_o.at[9 - c])
    for src, ss in sent:
        arrived(src, ss)
    for dx in (1, 3, 2):
        for dc in range(2):
            n = dx * 2 + dc - 1

            @pl.when(x + dx < 4)
            def _():
                for part in range(2):
                    arrived(kv.at[1, 8 + i, part], ss_own.at[1, n, part])

            @pl.when(x + dx >= 4)
            def _():
                arrived(cfw.at[0], ss_prev.at[1, n])

    @pl.loop(0, 8)
    def _(j):
        arrived(ob.at[j], ss_o.at[j])

    arrived(ob.at[8 + c], ss_o.at[9])


def body(outer, table, bq, bk, bv, gain, doc, wq, wk, wv):
    vmem = pl.BlockSpec(memory_space=pltpu.VMEM)
    anyw = pl.BlockSpec(memory_space=pl.ANY)
    dma = pltpu.SemaphoreType.DMA
    return pl.pallas_call(
        functools.partial(kernel, outer),
        out_shape=(
            jax.ShapeDtypeStruct((ROWS, HEADS * BASED_DIM), BF16),
            jax.ShapeDtypeStruct((ROWS, WIN_HEADS * HEAD_DIM), BF16),
        ),
        in_specs=[vmem] * 6 + [anyw] * 3,
        out_specs=(vmem, anyw),
        scratch_shapes=[
            pltpu.VMEM((2, 16, 2, 128, 128), BF16),
            pltpu.VMEM((2, 2, 128, 128), BF16),
            pltpu.VMEM((10, 128, 128), BF16),
            pltpu.VMEM((10, 128, 128), BF16),
            pltpu.VMEM((8, 8, 128), F32),
            pltpu.VMEM((BACK + 1, 8, 128), F32),
            pltpu.VMEM((16, 128), F32),
            pltpu.VMEM((8 * SLICE, 128), BF16),
            pltpu.VMEM((8, SLICE, 128), BF16),
            pltpu.VMEM((SLICE, 128), F32),
            pltpu.VMEM((BACK, SLICE, 128), F32),
            pltpu.VMEM((8, SLICE, 128), BF16),
            pltpu.VMEM((8 * SLICE, 128), BF16),
            pltpu.VMEM((PAIRS, 128, 128), F32),
            pltpu.VMEM((128, HEADS * 128), BF16),
            dma((2, 8, 2)), dma((2, 8, 2)), dma((2, 8)), dma((2, 8)),
            dma((10,)), dma((10,)), dma((10,)), dma((10,)), dma((2, 2)), dma((2, 2)),
            dma((8,)), dma((8,)), dma((BACK + 1,)), dma((BACK + 1,)),
            dma((8,)), dma((8,)), dma((BACK + 1,)), dma((BACK + 1,)), dma((8,)), dma((8,)),
        ],
        compiler_params=pltpu.CompilerParams(
            collective_id=0, has_side_effects=True, vmem_limit_bytes=40 << 20
        ),
        name="hybrid_attention",
    )(bq, bk, bv, gain.reshape(1, -1), doc.reshape(1, -1), jnp.asarray(table), wq, wk, wv)


def solution(mesh):
    tokens = P(("outer", "inner"), None)
    return jax.shard_map(
        functools.partial(body, mesh.shape["outer"], feature_table()),
        mesh=mesh,
        in_specs=(tokens, tokens, tokens, P(), P(("outer", "inner")), tokens, tokens, tokens),
        out_specs=(tokens, tokens),
        check_vma=False,
    )
```

time: 629 us -> 57 us (0.09)
  the two profiles are of different devices: /device:TPU:255 before, /device:TPU:1 now
where the time goes in v1:
time: 57 us; the launch traced here: 56.7 us
  Pallas kernels  48.4 us (85%)
  local copies, waits for them, and re-layouts  7.55 us (13%)
  between operations  0.68 us (1%)
    pallas_call x1, Pallas kernels, body(): pl.pallas_call(functools.partial(kernel, outer), out_shape=(jax.ShapeDtyp...  48.4 us
    unnamed x18, local copies, waits for them, and re-layouts  6.86 us

profile of v1, /device:TPU:1, one launch (start us, length us, event | category | flops | bytes accessed | tf_op | source)
XLA Modules:
  0.0 56.7 jit_solution(12372706077622429469)
XLA Ops:
  0.6 0.7 %reshape.10.gain = f32[1,640]{1,0:T(1,128)S(1)} reshape(f32[640]{0:T(1024)} %param.12) | data formatting | bytes 5120 | tf_op jit(solution)/shard_map/reshape | solution.py:413
  1.3 0.0 copy-start.6
  1.3 0.9 %copy.11.bq = bf16[128,110]{1,0:T(8,128)(2,1)S(1)} copy(bf16[128,110]{0,1:T(8,128)(2,1)} %param.9) | data formatting | bytes 56320 | tf_op args[0]
  2.2 0.0 copy-done.6
  2.2 0.0 copy-start.4
  2.2 0.0 copy-start.5
  2.2 0.1 copy.12.bk
  2.3 0.6 %copy-done.4 = f32[8,1280]{1,0:T(8,128)S(1)} copy-done((f32[8,1280]{1,0:T(8,128)S(1)}, f32[8,1280]{1,0:T(8,128)}, u32[]{:S(2)}) %copy-start.4) | copy-done | bytes 40984
  3.0 0.0 copy-done.5
  3.0 0.0 copy-start
  3.0 1.0 %copy-done = bf16[128,1280]{1,0:T(8,128)(2,1)S(1)} copy-done((bf16[128,1280]{1,0:T(8,128)(2,1)S(1)}, bf16[128,1280]{1,0:T(8,128)(2,1)}, u32[]{:S(2)}) %copy-start) | copy-done | bytes 327704
  4.0 0.0 copy-start.1
  4.0 1.0 %copy-done.1 = bf16[128,1280]{1,0:T(8,128)(2,1)S(1)} copy-done((bf16[128,1280]{1,0:T(8,128)(2,1)S(1)}, bf16[128,1280]{1,0:T(8,128)(2,1)}, u32[]{:S(2)}) %copy-start.1) | copy-done | bytes 327704
  4.9 0.0 copy-start.2
  4.9 1.0 %copy-done.2 = bf16[128,1280]{1,0:T(8,128)(2,1)S(1)} copy-done((bf16[128,1280]{1,0:T(8,128)(2,1)S(1)}, bf16[128,1280]{1,0:T(8,128)(2,1)}, u32[]{:S(2)}) %copy-start.2) | copy-done | bytes 327704
  5.9 0.0 copy-start.3
  5.9 0.9 %copy-done.3 = bf16[128,640]{1,0:T(8,128)(2,1)S(1)} copy-done((bf16[128,640]{1,0:T(8,128)(2,1)S(1)}, bf16[128,640]{1,0:T(8,128)(2,1)}, u32[]{:S(2)}) %copy-start.3) | copy-done | bytes 163864
  6.8 48.4 %hybrid_attention.1 = (bf16[128,640]{1,0:T(8,128)(2,1)S(1)}, bf16[128,1280]{1,0:T(8,128)(2,1)S(1)}) custom-call(bf16[128,110]{1,0:T(8,128)(2,1)S(1)} %copy.11.bq, bf16[128,110]{1,0:T(8,128)(2,1)S(1)} %copy.12.bk, bf16[128,640]{1,0:T(8,128)(2,1)S(1)} %copy-done.3, f32[1,640]{1,0:T(1,128)S(1)} %reshape.10.gain, s32[1,128]{1,0:T(1,128)S(1)} %bitcast.1, ...), custom_call_target="tpu_custom_call" | custom-call | tf_op jit(solution)/shard_map/hybrid_attention/pallas_call | solution.py:380
  55.3 0.7 %copy.15 = bf16[128,640]{1,0:T(8,128)(2,1)} copy(bf16[128,640]{1,0:T(8,128)(2,1)S(1)} %get-tuple-element.4) | data formatting | bytes 327680
  55.9 0.7 %copy.16 = bf16[128,1280]{1,0:T(8,128)(2,1)} copy(bf16[128,1280]{1,0:T(8,128)(2,1)S(1)} %get-tuple-element.5) | data formatting | bytes 655360
Async XLA Ops:
  1.3 0.9 %copy-start.6 = (bf16[128,110]{0,1:T(8,128)(2,1)S(1)}, bf16[128,110]{0,1:T(8,128)(2,1)}, u32[]{:S(2)}) copy-start(bf16[128,110]{0,1:T(8,128)(2,1)} %param.10) | copy-start | bytes 84484
  2.2 0.8 %copy-start.4 = (f32[8,1280]{1,0:T(8,128)S(1)}, f32[8,1280]{1,0:T(8,128)}, u32[]{:S(2)}) copy-start(f32[8,1280]{1,0:T(8,128)} %constant.2.clone.aux) | copy-start | bytes 122884
  2.2 0.8 %copy-start.5 = (s32[128]{0:T(128)S(1)}, s32[128]{0:T(128)}, u32[]{:S(2)}) copy-start(s32[128]{0:T(128)} %param.13) | copy-start | bytes 1540
  3.0 1.0 %copy-start = (bf16[128,1280]{1,0:T(8,128)(2,1)S(1)}, bf16[128,1280]{1,0:T(8,128)(2,1)}, u32[]{:S(2)}) copy-start(bf16[128,1280]{1,0:T(8,128)(2,1)} %wq.1) | copy-start | bytes 983044
  4.0 1.0 %copy-start.1 = (bf16[128,1280]{1,0:T(8,128)(2,1)S(1)}, bf16[128,1280]{1,0:T(8,128)(2,1)}, u32[]{:S(2)}) copy-start(bf16[128,1280]{1,0:T(8,128)(2,1)} %wk.1) | copy-start | bytes 983044
  4.9 1.0 %copy-start.2 = (bf16[128,1280]{1,0:T(8,128)(2,1)S(1)}, bf16[128,1280]{1,0:T(8,128)(2,1)}, u32[]{:S(2)}) copy-start(bf16[128,1280]{1,0:T(8,128)(2,1)} %wv.1) | copy-start | bytes 983044
  5.9 0.9 %copy-start.3 = (bf16[128,640]{1,0:T(8,128)(2,1)S(1)}, bf16[128,640]{1,0:T(8,128)(2,1)}, u32[]{:S(2)}) copy-start(bf16[128,640]{1,0:T(8,128)(2,1)} %bv.1) | copy-start | bytes 491524

commit v2 on v1

v2 whole, which is shorter than its diff:
```python
import functools
import math

import jax
import jax.numpy as jnp
import numpy as np
from jax import lax
from jax.experimental import pallas as pl
from jax.experimental.pallas import tpu as pltpu
from jax.sharding import PartitionSpec as P

HEADS = 10
BASED_DIM = 64
HEAD_DIM = 128
QK_DIM = 11
WIN_HEADS = 10
ROWS = 128
BACK = 8
FEAT = 80
PAIRS = HEADS // 2
SLICE = 64
MESSAGE = SLICE + 16
MESH = pl.DeviceIdType.MESH
ORDER = ((0, 1), (1, 0), (1, 1), (3, 0), (3, 1), (2, 0), (2, 1))
FAR = ORDER[1:]
NT = (((1,), (1,)), ((), ()))
TN = (((0,), (0,)), ((), ()))
F32 = jnp.float32
BF16 = jnp.bfloat16


def feature_table():
    table = np.zeros((8, HEADS * 128), np.float32)
    table[:2] = -1.0
    for head in range(HEADS):
        at = head * 128
        for a in range(QK_DIM + 1):
            for b in range(a, QK_DIM + 1):
                for row, entry in ((0, a), (1, b)):
                    if entry == 0:
                        table[row + 2, at] = 1.0
                    else:
                        table[row, at] = head * QK_DIM + entry - 1
                table[4, at] = 1.0 if a == b else 2.0
                at += 1
    return table


def kernel(
    outer,
    bq_hbm, bk_hbm, bv_hbm, gain_hbm, doc_hbm, aux_hbm, wq_hbm, wk_hbm, wv_hbm,
    bout, wout,
    bq, bk, bv, gain, doc, aux, wq, wk, wv,
    sq, skv, kv, cfw, qb, ob, d2, ssend, srecv, tsend, trecv, fsend, pf, tot, phq,
    ld, rs_own, ss_own, rs_prev, ss_prev, rs_q, ss_q, rs_o, ss_o, rs_c, ss_c,
    rs_s, ss_s, rs_t, ss_t, rs_f, ss_f,
):
    r = lax.axis_index("outer")
    i = lax.axis_index("inner")
    x = i // 2
    c = i % 2
    up = lax.rem(r + 1, outer)
    sib = x * 2 + (1 - c)

    loads = [
        pltpu.make_async_copy(src, dst, ld.at[n])
        for n, (src, dst) in enumerate(
            (
                (doc_hbm, doc), (bk_hbm, bk), (aux_hbm, aux), (bv_hbm, bv),
                (wk_hbm, wk), (wv_hbm, wv), (wq_hbm, wq), (bq_hbm, bq), (gain_hbm, gain),
            )
        )
    ]
    for load in loads:
        load.start()

    def to(dx, dc):
        return lax.rem(x + dx, 4) * 2 + lax.rem(c + dc, 2)

    def frm(dx, dc):
        return lax.rem(x + 4 - dx, 4) * 2 + lax.rem(c + dc, 2)

    def cols(ref, head):
        return ref.at[:, pl.ds(pl.multiple_of(head * HEAD_DIM, HEAD_DIM), HEAD_DIM)]

    def remote(src, dst, ss, rs, row, inner):
        return pltpu.make_async_remote_copy(
            src_ref=src, dst_ref=dst, send_sem=ss, recv_sem=rs,
            device_id=(row, inner), device_id_type=MESH,
        )

    def arrived(dst, rs):
        pltpu.make_async_copy(dst, dst, rs).wait()

    sent = []

    def send(src, dst, ss, rs, row, inner):
        remote(src, dst, ss, rs, row, inner).start()
        sent.append((src, ss))

    barrier = pltpu.get_barrier_semaphore()
    for dx, dc in ORDER:
        pl.semaphore_signal(barrier, inc=1, device_id=(r, to(dx, dc)), device_id_type=MESH)
    for k in range(1, BACK + 1):
        pl.semaphore_signal(
            barrier, inc=1, device_id=(lax.rem(r + outer - k, outer), i), device_id_type=MESH
        )

    for load in loads[:4]:
        load.wait()
    doc_row = doc[...].astype(F32)
    table = aux[...]
    place = lax.broadcasted_iota(jnp.int32, (QK_DIM * HEADS, HEADS * 128), 0).astype(F32)
    pick_a = jnp.where(place == table[0:1, :], 0.5, 0.0).astype(BF16)
    pick_b = jnp.where(place == table[1:2, :], 0.5, 0.0).astype(BF16)
    xk = bk[...]

    def features(proj):
        first = lax.dot_general(proj, pick_a, TN, preferred_element_type=F32) + table[2:3, :]
        second = lax.dot_general(proj, pick_b, TN, preferred_element_type=F32) + table[3:4, :]
        return first * second

    lane = lax.broadcasted_iota(jnp.int32, (128, 128), 1)
    row = lax.broadcasted_iota(jnp.int32, (128, 128), 0)
    left = lane < BASED_DIM
    own_rows = jnp.broadcast_to(doc_row, (128, 128))
    own_cols = own_rows.T
    keep = own_cols == doc_row[:, 127:128]
    fk = features(xk).astype(BF16)
    docs_tail = jnp.broadcast_to(doc_row, (16, 128)).astype(BF16)
    for p in range(PAIRS):
        vals = bv[:, p * 128 : (p + 1) * 128]
        kept = jnp.where(keep, vals.astype(F32), 0.0).astype(BF16)
        both = [
            lax.dot_general(
                fk[:, h * 128 : (h + 1) * 128], kept, TN, preferred_element_type=F32
            )
            for h in (2 * p, 2 * p + 1)
        ]
        state = jnp.where(left, both[0], both[1]).astype(BF16)
        for q in range(FEAT // 16):
            at = p * (FEAT // 16) + q
            ssend[at // 4, (at % 4) * 16 : (at % 4 + 1) * 16, :] = state[q * 16 : (q + 1) * 16]
    for at in range(PAIRS * FEAT // 16, 8 * SLICE // 16):
        ssend[at // 4, (at % 4) * 16 : (at % 4 + 1) * 16, :] = jnp.zeros((16, 128), BF16)
    for s in range(8):
        ssend[s, SLICE:MESSAGE, :] = docs_tail
    srecv[i] = ssend[i]

    for load in loads[4:6]:
        load.wait()
    for h in range(WIN_HEADS):
        skv[h, 0] = wk[:, h * 128 : (h + 1) * 128]
        skv[h, 1] = wv[:, h * 128 : (h + 1) * 128]

    pl.semaphore_wait(barrier, len(ORDER) + BACK)

    for n, (dx, dc) in enumerate(ORDER):
        d = to(dx, dc)
        send(ssend.at[d], srecv.at[i], ss_s.at[n], rs_s.at[i], r, d)
    send(skv.at[8:10], cfw, ss_c, rs_c, up, i)
    for n, (dx, dc) in enumerate(ORDER):
        d = to(dx, dc)
        send(skv.at[d], kv.at[0, 8 + i], ss_own.at[0, n], rs_own.at[0, i], r, d)
    send(skv.at[i], kv.at[0, i], ss_prev.at[0, i], rs_prev.at[0, i], up, i)
    for load in loads[6:]:
        load.wait()
    for h in range(WIN_HEADS):
        sq[h] = wq[:, h * 128 : (h + 1) * 128]
    send(sq.at[9 - c], qb.at[8 + c], ss_q.at[7], rs_q.at[8 + c], r, sib)
    send(skv.at[9 - c], kv.at[1, 8 + i], ss_own.at[1, 0], rs_own.at[1, i], r, sib)
    kv[0, 8 + i] = skv[i]
    kv[1, 8 + i] = skv[8 + c]
    qb[i] = sq[i]
    qb[8 + c] = sq[8 + c]

    sub = lax.broadcasted_iota(jnp.int32, (8, 128), 0)
    for dx, dc in ORDER:
        s = frm(dx, dc)
        arrived(srecv.at[s], rs_s.at[s])
    row_docs = jnp.zeros((8, 128), F32)
    for s in range(8):
        tail = srecv[s, SLICE:MESSAGE, :].astype(F32)
        row_docs = jnp.where(sub == s, tail[0:8], row_docs)
    last = [row_docs[s : s + 1, 127:128] for s in range(8)]
    acc = srecv[0, :SLICE, :].astype(F32)
    running = []
    for s in range(1, 8):
        running.append(acc)
        acc = srecv[s, :SLICE, :].astype(F32) + jnp.where(last[s] == last[s - 1], acc, 0.0)
    tsend[:SLICE, :] = acc.astype(BF16)
    tsend[SLICE:, :] = jnp.concatenate([row_docs, row_docs], axis=0).astype(BF16)
    for k in range(1, BACK + 1):
        send(tsend, trecv.at[k - 1], ss_t.at[k], rs_t.at[k], lax.rem(r + k, outer), i)

    arrived(cfw, rs_c)
    kv[1, i] = cfw[c]
    send(cfw.at[1 - c], kv.at[1, i], ss_prev.at[1, 0], rs_prev.at[1, i], r, sib)
    for n, (dx, dc) in enumerate(FAR):
        h = lax.rem(c + dc, 2)
        d = to(dx, dc)

        @pl.when(x + dx < 4)
        def _():
            remote(
                skv.at[8 + h], kv.at[1, 8 + i], ss_own.at[1, n + 1], rs_own.at[1, i], r, d
            ).start()

        @pl.when(x + dx >= 4)
        def _():
            remote(
                cfw.at[h], kv.at[1, i], ss_prev.at[1, n + 1], rs_prev.at[1, i], r, d
            ).start()

    for n, (dx, dc) in enumerate(ORDER):
        s = frm(dx, dc)
        arrived(kv.at[0, 8 + s], rs_own.at[0, s])
        send(kv.at[0, 8 + s], kv.at[0, s], ss_prev.at[0, s], rs_prev.at[0, s], up, i)
    for n, (dx, dc) in enumerate(ORDER):
        d = to(dx, dc)
        send(sq.at[d], qb.at[i], ss_q.at[n], rs_q.at[i], r, d)

    before = []
    for k in range(1, BACK + 1):
        arrived(trecv.at[k - 1], rs_t.at[k])
        before.append(trecv[k - 1, SLICE:MESSAGE, :].astype(F32)[0:8])
    entering_doc = jnp.where(r >= 1, before[0][7:8, 127:128], -1.0)
    enter = jnp.zeros((SLICE, 128), F32)
    for k in range(1, BACK + 1):
        same = jnp.where(r >= k, before[k - 1][7:8, 127:128], -2.0) == entering_doc
        enter = enter + jnp.where(same, trecv[k - 1, :SLICE, :].astype(F32), 0.0)
    fsend[0] = enter.astype(BF16)
    for s in range(1, 8):
        fsend[s] = (running[s - 1] + jnp.where(last[s - 1] == entering_doc, enter, 0.0)).astype(BF16)

    def block(ref, d):
        return ref.at[pl.ds(pl.multiple_of(d * SLICE, SLICE), SLICE)]

    for n, (dx, dc) in enumerate(ORDER):
        d = to(dx, dc)
        send(fsend.at[d], block(pf, i), ss_f.at[n], rs_f.at[i], r, d)
    pf[pl.ds(pl.multiple_of(i * SLICE, SLICE), SLICE), :] = fsend[i]
    d2[0:8] = jnp.where(r >= 1, before[0], -1.0)
    d2[8:16] = row_docs

    xq = bq[...]
    inside = (own_cols == own_rows) & (lane <= row)
    lane_q = lax.broadcasted_iota(jnp.int32, (QK_DIM * HEADS, 128), 0)
    for p in range(PAIRS):
        vals = bv[:, p * 128 : (p + 1) * 128]
        both = []
        for h in (2 * p, 2 * p + 1):
            mine = (lane_q >= h * QK_DIM) & (lane_q < (h + 1) * QK_DIM)
            part_q = jnp.where(mine, xq.astype(F32), 0.0).astype(BF16)
            dots = lax.dot_general(part_q, xk, TN, preferred_element_type=F32) * 0.25 + 1.0
            weight = jnp.where(inside, dots * dots, 0.0).astype(BF16)
            both.append(jnp.dot(weight, vals, preferred_element_type=F32))
        tot[p] = jnp.where(left, both[0], both[1])
    phq[...] = (features(xq) * table[4:5, :]).astype(BF16)

    factor = math.log2(math.e) / math.sqrt(HEAD_DIM)

    def attend(b, j, at):
        query = qb[at]
        docq = jnp.broadcast_to(d2[pl.ds(8 + j, 1), :], (128, 128)).T
        scores = []
        top = None
        for t in range(BACK + 1):
            block_scores = lax.dot_general(
                query, kv[b, j + t, 0], NT, preferred_element_type=F32
            )
            see = docq == d2[pl.ds(j + t, 1), :]
            if t == 0:
                see = see & (lane > row)
            if t == BACK:
                see = see & (lane <= row)
            block_scores = jnp.where(see, block_scores, -1e30)
            scores.append(block_scores)
            top = block_scores if top is None else jnp.maximum(top, block_scores)
        peak = jnp.max(top, axis=1, keepdims=True)
        whole = None
        mixed = None
        for t in range(BACK + 1):
            prob = jnp.exp2((scores[t] - peak) * factor)
            whole = prob if whole is None else whole + prob
            term = jnp.dot(prob.astype(BF16), kv[b, j + t, 1], preferred_element_type=F32)
            mixed = term if mixed is None else mixed + term
        rowsum = jnp.sum(whole, axis=1, keepdims=True)
        ob[at] = (mixed / rowsum).astype(BF16)

    arrived(qb.at[9 - c], rs_q.at[9 - c])

    @pl.loop(0, 2 * x + 2)
    def _(s):
        @pl.when(s != i)
        def _():
            arrived(kv.at[1, 8 + s], rs_own.at[1, s])

    @pl.loop(2 * x, 8)
    def _(s):
        @pl.when(s != i)
        def _():
            arrived(kv.at[1, s], rs_prev.at[1, s])

    @pl.loop(0, 2)
    def _(core):
        attend(1, 2 * x + core, 8 + core)

    send(ob.at[9 - c], cols(wout, 8 + c), ss_o.at[8], rs_o.at[8 + c], r, sib)
    pltpu.make_async_copy(ob.at[8 + c], cols(wout, 8 + c), ss_o.at[9]).start()

    @pl.loop(0, 8)
    def _(step):
        j = 7 - step

        @pl.when(j != i)
        def _():
            arrived(qb.at[j], rs_q.at[j])

        arrived(kv.at[0, j], rs_prev.at[0, j])
        attend(0, j, j)

        @pl.when(j != i)
        def _():
            remote(ob.at[j], cols(wout, i), ss_o.at[j], rs_o.at[i], r, j).start()

        @pl.when(j == i)
        def _():
            pltpu.make_async_copy(ob.at[j], cols(wout, i), ss_o.at[j]).start()

    for dx, dc in ORDER:
        s = frm(dx, dc)
        arrived(block(pf, s), rs_f.at[s])
    previous = jnp.where(i == 0, entering_doc, -1.0)
    for s in range(1, 8):
        previous = jnp.where(i == s, last[s - 1], previous)
    carried = own_cols == previous
    rest = jnp.zeros((128 - FEAT, 128), BF16)
    for p in range(PAIRS):
        state = jnp.concatenate([pf[p * FEAT : (p + 1) * FEAT, :], rest], axis=0)
        both = [
            jnp.dot(phq[:, h * 128 : (h + 1) * 128], state, preferred_element_type=F32)
            for h in (2 * p, 2 * p + 1)
        ]
        total = tot[p] + jnp.where(carried, jnp.where(left, both[0], both[1]), 0.0)
        square = total * total
        one = jnp.sum(jnp.where(left, square, 0.0), axis=1, keepdims=True)
        two = jnp.sum(jnp.where(left, 0.0, square), axis=1, keepdims=True)
        mean = jnp.where(left, one, two) * (1.0 / BASED_DIM)
        scaled = total * lax.rsqrt(mean + 1e-5) * gain[p * 128 : (p + 1) * 128].reshape(1, 128)
        bout[:, p * 128 : (p + 1) * 128] = scaled.astype(BF16)

    @pl.loop(0, 8)
    def _(j):
        @pl.when(j != i)
        def _():
            arrived(cols(wout, j), rs_o.at[j])

    arrived(cols(wout, 9 - c), rs_o.at[9 - c])
    for src, ss in sent:
        arrived(src, ss)
    for n, (dx, dc) in enumerate(FAR):

        @pl.when(x + dx < 4)
        def _():
            arrived(kv.at[1, 8 + i], ss_own.at[1, n + 1])

        @pl.when(x + dx >= 4)
        def _():
            arrived(cfw.at[0], ss_prev.at[1, n + 1])

    @pl.loop(0, 8)
    def _(j):
        arrived(ob.at[j], ss_o.at[j])

    arrived(ob.at[8 + c], ss_o.at[9])


def body(outer, table, bq, bk, bv, gain, doc, wq, wk, wv):
    vmem = pl.BlockSpec(memory_space=pltpu.VMEM)
    anyw = pl.BlockSpec(memory_space=pl.ANY)
    dma = pltpu.SemaphoreType.DMA
    operands = (bq.T, bk.T, bv, gain, doc.reshape(1, -1), jnp.asarray(table), wq, wk, wv)
    return pl.pallas_call(
        functools.partial(kernel, outer),
        out_shape=(
            jax.ShapeDtypeStruct((ROWS, HEADS * BASED_DIM), BF16),
            jax.ShapeDtypeStruct((ROWS, WIN_HEADS * HEAD_DIM), BF16),
        ),
        in_specs=[anyw] * 9,
        out_specs=(vmem, anyw),
        scratch_shapes=[pltpu.VMEM(a.shape, a.dtype) for a in operands]
        + [
            pltpu.VMEM((10, 128, 128), BF16),
            pltpu.VMEM((10, 2, 128, 128), BF16),
            pltpu.VMEM((2, 16, 2, 128, 128), BF16),
            pltpu.VMEM((2, 2, 128, 128), BF16),
            pltpu.VMEM((10, 128, 128), BF16),
            pltpu.VMEM((10, 128, 128), BF16),
            pltpu.VMEM((16, 128), F32),
            pltpu.VMEM((8, MESSAGE, 128), BF16),
            pltpu.VMEM((8, MESSAGE, 128), BF16),
            pltpu.VMEM((MESSAGE, 128), BF16),
            pltpu.VMEM((BACK, MESSAGE, 128), BF16),
            pltpu.VMEM((8, SLICE, 128), BF16),
            pltpu.VMEM((8 * SLICE, 128), BF16),
            pltpu.VMEM((PAIRS, 128, 128), F32),
            pltpu.VMEM((128, HEADS * 128), BF16),
            dma((9,)), dma((2, 8)), dma((2, 8)), dma((2, 8)), dma((2, 8)),
            dma((10,)), dma((10,)), dma((10,)), dma((10,)), dma, dma,
            dma((8,)), dma((8,)), dma((BACK + 1,)), dma((BACK + 1,)), dma((8,)), dma((8,)),
        ],
        compiler_params=pltpu.CompilerParams(
            collective_id=0, has_side_effects=True, vmem_limit_bytes=60 << 20
        ),
        name="hybrid_attention",
    )(*operands)


def solution(mesh):
    tokens = P(("outer", "inner"), None)
    return jax.shard_map(
        functools.partial(body, mesh.shape["outer"], feature_table()),
        mesh=mesh,
        in_specs=(tokens, tokens, tokens, P(), P(("outer", "inner")), tokens, tokens, tokens),
        out_specs=(tokens, tokens),
        check_vma=False,
    )
```

time: 57 us -> 46.7 us (0.82)
  local copies, waits for them, and re-layouts: 7.55 us -> 2.37 us
  Pallas kernels: 48.4 us -> 43.5 us
    pallas_call x1, Pallas kernels: 48.4 us -> 43.5 us  [body(): pl.pallas_call(functools.partial(kernel, outer), out_shape=(jax.ShapeDtyp...]
    unnamed x18 -> x4, local copies, waits for them, and re-layouts: 6.86 us -> 2.37 us
    reshape x1 -> x0, local copies, waits for them, and re-layouts: 0.69 us -> none  [body(): gain.reshape(1, -1)]
where the time goes in v2:
time: 46.7 us; the launch traced here: 46.5 us
  Pallas kernels  43.5 us (93%)
  local copies, waits for them, and re-layouts  2.37 us (5%)
  between operations  0.65 us (1%)
    pallas_call x1, Pallas kernels, body(): pl.pallas_call(functools.partial(kernel, outer), out_shape=(jax.ShapeDtyp...  43.5 us
    unnamed x4, local copies, waits for them, and re-layouts  2.37 us

profile of v2, /device:TPU:1, one launch (start us, length us, event | category | flops | bytes accessed | tf_op | source)
XLA Modules:
  0.0 46.5 jit_solution(13376246309546144984)
XLA Ops:
  0.6 43.5 %hybrid_attention.1 = (bf16[128,640]{1,0:T(8,128)(2,1)}, bf16[128,1280]{1,0:T(8,128)(2,1)}) custom-call(bf16[110,128]{1,0:T(8,128)(2,1)} %bitcast.3, bf16[110,128]{1,0:T(8,128)(2,1)} %bitcast.4, bf16[128,640]{1,0:T(8,128)(2,1)} %bv_hbm.1, f32[640]{0:T(1024)} %gain_hbm.1, s32[1,128]{1,0:T(1,128)} %bitcast.5, f32[8,1280]{1,0:T(8,128)} %constant.2.clone.aux_hbm, ...), custom_call_target="tpu_custom_call" | custom-call | tf_op jit(solution)/shard_map/hybrid_attention/pallas_call | solution.py:384
  44.2 0.0 copy-start
  44.2 1.6 %copy.13 = bf16[128,640]{1,0:T(8,128)(2,1)} copy(bf16[128,640]{1,0:T(8,128)(2,1)} %get-tuple-element.4) | data formatting | bytes 327680
  45.8 0.0 copy-done
  45.8 0.7 %copy.14 = bf16[128,1280]{1,0:T(8,128)(2,1)} copy(bf16[128,1280]{1,0:T(8,128)(2,1)S(1)} %copy-done) | data formatting | bytes 655360
Async XLA Ops:
  44.2 1.7 %copy-start = (bf16[128,1280]{1,0:T(8,128)(2,1)S(1)}, bf16[128,1280]{1,0:T(8,128)(2,1)}, u32[]{:S(2)}) copy-start(bf16[128,1280]{1,0:T(8,128)(2,1)} %get-tuple-element.5) | copy-start | bytes 983044

commit v3 on v2

v3 whole, which is shorter than its diff:
```python
import functools
import math

import jax
import jax.numpy as jnp
import numpy as np
from jax import lax
from jax.experimental import pallas as pl
from jax.experimental.pallas import tpu as pltpu
from jax.sharding import PartitionSpec as P

HEADS = 10
BASED_DIM = 64
HEAD_DIM = 128
QK_DIM = 11
WIN_HEADS = 10
ROWS = 128
BACK = 8
PLANE = 4
PAIRS = HEADS // 2
GROUP = 13
GROUPS = 6
FEAT = GROUPS * 16
PLANE_DEVS = 32
MESH = pl.DeviceIdType.MESH
ORDER = ((0, 1), (1, 0), (1, 1), (3, 0), (3, 1), (2, 0), (2, 1))
FAR = ORDER[1:]
NT = (((1,), (1,)), ((), ()))
TN = (((0,), (0,)), ((), ()))
F32 = jnp.float32
BF16 = jnp.bfloat16


def feature_table():
    table = np.zeros((8, HEADS * 128), np.float32)
    table[:2] = -1.0
    for head in range(HEADS):
        feature = 0
        for a in range(QK_DIM + 1):
            for b in range(a, QK_DIM + 1):
                at = head * 128 + feature // GROUP * 16 + feature % GROUP
                for row, entry in ((0, a), (1, b)):
                    if entry == 0:
                        table[row + 2, at] = 1.0
                    else:
                        table[row, at] = head * QK_DIM + entry - 1
                table[4, at] = 1.0 if a == b else 2.0
                feature += 1
    return table


def kernel(
    outer,
    bq_hbm, bk_hbm, bv_hbm, gain_hbm, doc_hbm, aux_hbm, wq_hbm, wk_hbm, wv_hbm,
    bout, wout,
    bq, bk, bv, gain, doc, aux, wq, wk, wv,
    sq, skv, kv, cfw, qb, ob, d2, ssend, srecv, running, plane_docs, wsend, wrecv, fsend, pf, tot, phq,
    peaks, sums, mixes,
    ld, rs_own, ss_own, rs_prev, ss_prev, rs_q, ss_q, rs_o, ss_o, rs_c, ss_c,
    rs_s, ss_s, rs_w, ss_w, rs_f, ss_f,
):
    r = lax.axis_index("outer")
    i = lax.axis_index("inner")
    x = i // 2
    c = i % 2
    z = r // PLANE
    y = r % PLANE
    me = y * 8 + i
    up = lax.rem(r + 1, outer)
    sib = x * 2 + (1 - c)

    loads = [
        pltpu.make_async_copy(src, dst, ld.at[n])
        for n, (src, dst) in enumerate(
            (
                (doc_hbm, doc), (bk_hbm, bk), (aux_hbm, aux), (bv_hbm, bv),
                (wk_hbm, wk), (wv_hbm, wv), (wq_hbm, wq), (bq_hbm, bq), (gain_hbm, gain),
            )
        )
    ]
    for load in loads:
        load.start()

    def to(dx, dc):
        return lax.rem(x + dx, 4) * 2 + lax.rem(c + dc, 2)

    plane_rows = [lax.rem(y + k, PLANE) for k in range(PLANE)]
    plane_outer = [z * PLANE + k for k in plane_rows]
    plane_inner = [lax.rem(i + k, 8) for k in range(8)]
    others = [
        (plane_rows[n // 8] * 8 + plane_inner[n % 8], plane_outer[n // 8], plane_inner[n % 8])
        for n in range(1, PLANE_DEVS)
    ]

    def frm(dx, dc):
        return lax.rem(x + 4 - dx, 4) * 2 + lax.rem(c + dc, 2)

    def cols(ref, head):
        return ref.at[:, pl.ds(pl.multiple_of(head * HEAD_DIM, HEAD_DIM), HEAD_DIM)]

    def remote(src, dst, ss, rs, row, inner):
        return pltpu.make_async_remote_copy(
            src_ref=src, dst_ref=dst, send_sem=ss, recv_sem=rs,
            device_id=(row, inner), device_id_type=MESH,
        )

    def arrived(dst, rs):
        pltpu.make_async_copy(dst, dst, rs).wait()

    sent = []

    def send(src, dst, ss, rs, row, inner):
        remote(src, dst, ss, rs, row, inner).start()
        sent.append((src, ss))

    barrier = pltpu.get_barrier_semaphore()
    for dx, dc in ORDER:
        pl.semaphore_signal(barrier, inc=1, device_id=(r, to(dx, dc)), device_id_type=MESH)
    senders = [lax.rem(r + outer - 1, outer)]
    senders += [lax.rem(r + outer - k * PLANE, outer) for k in (1, 2)]
    for other in senders:
        pl.semaphore_signal(barrier, inc=1, device_id=(other, i), device_id_type=MESH)

    for _, row, inner in others[7:]:
        pl.semaphore_signal(barrier, inc=1, device_id=(row, inner), device_id_type=MESH)


    for load in loads[:4]:
        load.wait()
    doc_row = doc[...].astype(F32)
    table = aux[...]
    place = lax.broadcasted_iota(jnp.int32, (QK_DIM * HEADS, HEADS * 128), 0).astype(F32)
    pick_a = jnp.where(place == table[0:1, :], 0.5, 0.0).astype(BF16)
    pick_b = jnp.where(place == table[1:2, :], 0.5, 0.0).astype(BF16)
    xk = bk[...]

    def features(proj):
        first = lax.dot_general(proj, pick_a, TN, preferred_element_type=F32) + table[2:3, :]
        second = lax.dot_general(proj, pick_b, TN, preferred_element_type=F32) + table[3:4, :]
        return first * second

    lane = lax.broadcasted_iota(jnp.int32, (128, 128), 1)
    row = lax.broadcasted_iota(jnp.int32, (128, 128), 0)
    left = lane < BASED_DIM
    own_rows = jnp.broadcast_to(doc_row, (128, 128))
    own_cols = own_rows.T
    keep = own_cols == doc_row[:, 127:128]
    fk = features(xk).astype(BF16)
    docs_tail = jnp.broadcast_to(doc_row, (16, 128))
    tail = lax.broadcasted_iota(jnp.int32, (16, 128), 0) >= GROUP
    for p in range(PAIRS):
        vals = bv[:, p * 128 : (p + 1) * 128]
        kept = jnp.where(keep, vals.astype(F32), 0.0).astype(BF16)
        both = [
            lax.dot_general(
                fk[:, h * 128 : (h + 1) * 128], kept, TN, preferred_element_type=F32
            )
            for h in (2 * p, 2 * p + 1)
        ]
        state = jnp.where(left, both[0], both[1])
        for q in range(GROUPS):
            ssend[p * GROUPS + q] = jnp.where(
                tail, docs_tail, state[q * 16 : (q + 1) * 16]
            ).astype(BF16)
    for q in range(PAIRS * GROUPS, PLANE_DEVS):
        ssend[q] = docs_tail.astype(BF16)
    srecv[me] = ssend[me]

    for load in loads[4:6]:
        load.wait()
    for h in range(WIN_HEADS):
        skv[h, 0] = wk[:, h * 128 : (h + 1) * 128]
        skv[h, 1] = wv[:, h * 128 : (h + 1) * 128]

    pl.semaphore_wait(barrier, PLANE_DEVS - 1 + len(senders))

    for n, (place, outer_at, inner_at) in enumerate(others):
        remote(ssend.at[place], srecv.at[me], ss_s.at[n], rs_s.at[me], outer_at, inner_at).start()
    send(skv.at[8:10], cfw, ss_c, rs_c, up, i)
    send(skv.at[i], kv.at[0, i], ss_prev.at[0, i], rs_prev.at[0, i], up, i)

    def send_kv(steps):
        for n in steps:
            d = to(*ORDER[n])
            send(skv.at[d], kv.at[0, 8 + i], ss_own.at[0, n], rs_own.at[0, i], r, d)

    def pass_on(steps):
        for n in steps:
            s = frm(*ORDER[n])
            arrived(kv.at[0, 8 + s], rs_own.at[0, s])
            send(kv.at[0, 8 + s], kv.at[0, s], ss_prev.at[0, s], rs_prev.at[0, s], up, i)

    send_kv(range(5))
    for load in loads[6:]:
        load.wait()
    for h in range(WIN_HEADS):
        sq[h] = wq[:, h * 128 : (h + 1) * 128]
    send(sq.at[9 - c], qb.at[8 + c], ss_q.at[7], rs_q.at[8 + c], r, sib)
    send(skv.at[9 - c], kv.at[1, 8 + i], ss_own.at[1, 0], rs_own.at[1, i], r, sib)
    kv[0, 8 + i] = skv[i]
    kv[1, 8 + i] = skv[8 + c]
    qb[i] = sq[i]
    qb[8 + c] = sq[8 + c]

    pass_on(range(1))

    for place, _, _ in others:
        arrived(srecv.at[place], rs_s.at[place])

    messages = [srecv[k].astype(F32) for k in range(PLANE_DEVS)]
    last = [message[GROUP : GROUP + 1, 127:128] for message in messages]
    acc = messages[0]
    for k in range(1, PLANE_DEVS):
        running[k] = acc
        acc = messages[k] + jnp.where(last[k] == last[k - 1], acc, 0.0)
    sub = lax.broadcasted_iota(jnp.int32, (8, 128), 0)
    for k in range(PLANE):
        docs = jnp.zeros((8, 128), F32)
        for m in range(8):
            docs = jnp.where(sub == m, messages[k * 8 + m][GROUP : GROUP + 1, :], docs)
        plane_docs[k] = docs
    wsend[:16, :] = acc.astype(BF16)
    wsend[16:, :] = jnp.concatenate([docs, docs], axis=0).astype(BF16)
    for k in (1, 2):
        send(wsend, wrecv.at[k - 1], ss_w.at[k], rs_w.at[k], lax.rem(r + k * PLANE, outer), i)

    send_kv(range(5, 7))
    arrived(cfw, rs_c)
    kv[1, i] = cfw[c]
    send(cfw.at[1 - c], kv.at[1, i], ss_prev.at[1, 0], rs_prev.at[1, i], r, sib)
    pass_on(range(1, 5))
    for n, (dx, dc) in enumerate(ORDER):
        d = to(dx, dc)
        send(sq.at[d], qb.at[i], ss_q.at[n], rs_q.at[i], r, d)

    for n, (dx, dc) in enumerate(FAR):
        h = lax.rem(c + dc, 2)
        d = to(dx, dc)

        @pl.when(x + dx < 4)
        def _():
            remote(
                skv.at[8 + h], kv.at[1, 8 + i], ss_own.at[1, n + 1], rs_own.at[1, i], r, d
            ).start()

        @pl.when(x + dx >= 4)
        def _():
            remote(
                cfw.at[h], kv.at[1, i], ss_prev.at[1, n + 1], rs_prev.at[1, i], r, d
            ).start()

    pass_on(range(5, 7))

    xq = bq[...]
    inside = (own_cols == own_rows) & (lane <= row)
    lane_q = lax.broadcasted_iota(jnp.int32, (QK_DIM * HEADS, 128), 0)
    for p in range(PAIRS):
        vals = bv[:, p * 128 : (p + 1) * 128]
        both = []
        for h in (2 * p, 2 * p + 1):
            mine = (lane_q >= h * QK_DIM) & (lane_q < (h + 1) * QK_DIM)
            part_q = jnp.where(mine, xq.astype(F32), 0.0).astype(BF16)
            dots = lax.dot_general(part_q, xk, TN, preferred_element_type=F32) * 0.25 + 1.0
            weight = jnp.where(inside, dots * dots, 0.0).astype(BF16)
            both.append(jnp.dot(weight, vals, preferred_element_type=F32))
        tot[p] = jnp.where(left, both[0], both[1])
    phq[...] = (features(xq) * table[4:5, :]).astype(BF16)

    factor = math.log2(math.e) / math.sqrt(HEAD_DIM)
    own_docs = plane_docs[y]
    for k in range(8):
        d2[:, (8 + k) * 128 : (9 + k) * 128] = own_docs[k : k + 1]

    def doc_span(slot, count):
        return d2[:, pl.ds(pl.multiple_of(slot * 128, 128), count * 128)]

    def weigh(query, b, slot, count, low, high, start):
        docq = jnp.broadcast_to(query[1], (128, 128)).T[:, 0:1]
        keys = kv[b, pl.ds(slot, count), 0].reshape(count * 128, 128)
        scores = lax.dot_general(query[0], keys, NT, preferred_element_type=F32)
        off = lax.broadcasted_iota(jnp.int32, scores.shape, 1) - lax.broadcasted_iota(
            jnp.int32, scores.shape, 0
        )
        see = docq == doc_span(slot, count)
        if low is not None:
            see = see & (off > low)
        if high is not None:
            see = see & (off <= high)
        scores = jnp.where(see, scores, -1e30)
        peak = jnp.max(scores, axis=1, keepdims=True)
        if start is not None:
            peak = jnp.maximum(peak, start)
        prob = jnp.exp2((scores - peak) * factor)
        rowsum = jnp.sum(prob, axis=1, keepdims=True)
        values = kv[b, pl.ds(slot, count), 1].reshape(count * 128, 128)
        mixed = jnp.dot(prob.astype(BF16), values, preferred_element_type=F32)
        return peak, rowsum, mixed

    def attend(b, j, at):
        _, rowsum, mixed = weigh(
            (qb[at], doc_span(8 + j, 1)), b, j, BACK + 1, 0, BACK * 128, None
        )
        ob[at] = (mixed / rowsum).astype(BF16)

    def own_part(j, count):
        peak, rowsum, mixed = weigh(
            (qb[j], doc_span(8 + j, 1)), 0, 8, count, None, j * 128, None
        )
        peaks[j] = jnp.broadcast_to(peak, (128, 128))
        sums[j] = jnp.broadcast_to(rowsum, (128, 128))
        mixes[j] = mixed

    def last_part(j, first):
        before = peaks[j]
        peak, rowsum, mixed = weigh(
            (qb[j], doc_span(8 + j, 1)), 0, first, 8 - first, (j - first) * 128, None,
            before[:, 0:1],
        )
        fade = jnp.exp2((before - peak) * factor)
        ob[j] = ((mixed + mixes[j] * fade) / (rowsum + sums[j] * fade)).astype(BF16)

    for dx, dc in ORDER:
        s = frm(dx, dc)
        arrived(qb.at[s], rs_q.at[s])

    @pl.loop(4, 8)
    def _(j):
        own_part(j, 8)

    @pl.loop(0, 4)
    def _(j):
        own_part(j, 4)

    for k in (1, 2):
        arrived(wrecv.at[k - 1], rs_w.at[k])
    before = [wrecv[k].astype(F32) for k in range(2)]
    entering_doc = jnp.where(z >= 1, before[0][23:24, 127:128], -1.0)
    enter = jnp.where(z >= 1, before[0][:16], 0.0)
    same = jnp.where(z >= 2, before[1][23:24, 127:128], -2.0) == entering_doc
    enter = enter + jnp.where(same, before[1][:16], 0.0)
    fsend[0] = enter.astype(BF16)
    previous = entering_doc
    for k in range(1, PLANE_DEVS):
        fsend[k] = (running[k] + jnp.where(last[k - 1] == entering_doc, enter, 0.0)).astype(BF16)
        previous = jnp.where(me == k, last[k - 1], previous)

    for n, (place, outer_at, inner_at) in enumerate(others):
        remote(fsend.at[place], pf.at[me], ss_f.at[n], rs_f.at[me], outer_at, inner_at).start()
    pf[me] = fsend[me]
    docs_before = jnp.where(z >= 1, before[0][16:24], -1.0)
    docs_before = jnp.where(y >= 1, plane_docs[jnp.maximum(y - 1, 0)], docs_before)
    for k in range(8):
        d2[:, k * 128 : (k + 1) * 128] = docs_before[k : k + 1]

    def finish(j):
        @pl.when(j != i)
        def _():
            remote(ob.at[j], cols(wout, i), ss_o.at[j], rs_o.at[i], r, j).start()

        @pl.when(j == i)
        def _():
            pltpu.make_async_copy(ob.at[j], cols(wout, i), ss_o.at[j]).start()

    @pl.loop(0, 4)
    def _(step):
        arrived(kv.at[0, 7 - step], rs_prev.at[0, 7 - step])

    @pl.loop(0, 4)
    def _(step):
        last_part(7 - step, 4)
        finish(7 - step)

    @pl.loop(0, 4)
    def _(step):
        arrived(kv.at[0, 3 - step], rs_prev.at[0, 3 - step])

    @pl.loop(0, 4)
    def _(step):
        last_part(3 - step, 0)
        finish(3 - step)

    arrived(qb.at[9 - c], rs_q.at[9 - c])

    @pl.loop(0, 2 * x + 2)
    def _(s):
        @pl.when(s != i)
        def _():
            arrived(kv.at[1, 8 + s], rs_own.at[1, s])

    @pl.loop(2 * x, 8)
    def _(s):
        @pl.when(s != i)
        def _():
            arrived(kv.at[1, s], rs_prev.at[1, s])

    @pl.loop(0, 2)
    def _(step):
        core = lax.rem(1 - c + step, 2)
        attend(1, 2 * x + core, 8 + core)

        @pl.when(step == 0)
        def _():
            remote(ob.at[9 - c], cols(wout, 8 + c), ss_o.at[8], rs_o.at[8 + c], r, sib).start()

    pltpu.make_async_copy(ob.at[8 + c], cols(wout, 8 + c), ss_o.at[9]).start()

    for place, _, _ in others:
        arrived(pf.at[place], rs_f.at[place])

    carried = own_cols == previous
    for p in range(PAIRS):
        state = pf[p * GROUPS : (p + 1) * GROUPS].reshape(FEAT, 128)
        both = [
            jnp.dot(phq[:, h * 128 : h * 128 + FEAT], state, preferred_element_type=F32)
            for h in (2 * p, 2 * p + 1)
        ]
        total = tot[p] + jnp.where(carried, jnp.where(left, both[0], both[1]), 0.0)
        square = total * total
        one = jnp.sum(jnp.where(left, square, 0.0), axis=1, keepdims=True)
        two = jnp.sum(jnp.where(left, 0.0, square), axis=1, keepdims=True)
        mean = jnp.where(left, one, two) * (1.0 / BASED_DIM)
        scaled = total * lax.rsqrt(mean + 1e-5) * gain[p * 128 : (p + 1) * 128].reshape(1, 128)
        bout[:, p * 128 : (p + 1) * 128] = scaled.astype(BF16)

    @pl.loop(0, 8)
    def _(j):
        @pl.when(j != i)
        def _():
            arrived(cols(wout, j), rs_o.at[j])

    arrived(cols(wout, 9 - c), rs_o.at[9 - c])
    for src, ss in sent:
        arrived(src, ss)

    @pl.loop(0, PLANE_DEVS - 1)
    def _(n):
        arrived(ssend.at[0], ss_s.at[n])
        arrived(fsend.at[0], ss_f.at[n])

    for n, (dx, dc) in enumerate(FAR):

        @pl.when(x + dx < 4)
        def _():
            arrived(kv.at[1, 8 + i], ss_own.at[1, n + 1])

        @pl.when(x + dx >= 4)
        def _():
            arrived(cfw.at[0], ss_prev.at[1, n + 1])

    @pl.loop(0, 8)
    def _(j):
        arrived(ob.at[j], ss_o.at[j])

    arrived(ob.at[9 - c], ss_o.at[8])
    arrived(ob.at[8 + c], ss_o.at[9])


def hand_over(based, window, bout, wout, held_based, held_window, sems):
    loads = [
        pltpu.make_async_copy(window, held_window, sems.at[0]),
        pltpu.make_async_copy(based, held_based, sems.at[1]),
    ]
    stores = [
        pltpu.make_async_copy(held_window, wout, sems.at[2]),
        pltpu.make_async_copy(held_based, bout, sems.at[3]),
    ]
    for load in loads:
        load.start()
    for load, store in zip(loads, stores):
        load.wait()
        store.start()
    for store in stores:
        store.wait()


def body(outer, table, bq, bk, bv, gain, doc, wq, wk, wv):
    vmem = pl.BlockSpec(memory_space=pltpu.VMEM)
    anyw = pl.BlockSpec(memory_space=pl.ANY)
    dma = pltpu.SemaphoreType.DMA
    operands = (bq.T, bk.T, bv, gain, doc.reshape(1, -1), jnp.asarray(table), wq, wk, wv)
    parts = pl.pallas_call(
        functools.partial(kernel, outer),
        out_shape=(
            jax.ShapeDtypeStruct((ROWS, HEADS * BASED_DIM), BF16),
            jax.ShapeDtypeStruct((ROWS, WIN_HEADS * HEAD_DIM), BF16),
        ),
        in_specs=[anyw] * 9,
        out_specs=(vmem, anyw),
        scratch_shapes=[pltpu.VMEM(a.shape, a.dtype) for a in operands]
        + [
            pltpu.VMEM((10, 128, 128), BF16),
            pltpu.VMEM((10, 2, 128, 128), BF16),
            pltpu.VMEM((2, 16, 2, 128, 128), BF16),
            pltpu.VMEM((2, 2, 128, 128), BF16),
            pltpu.VMEM((10, 128, 128), BF16),
            pltpu.VMEM((10, 128, 128), BF16),
            pltpu.VMEM((1, 16 * 128), F32),
            pltpu.VMEM((PLANE_DEVS, 16, 128), BF16),
            pltpu.VMEM((PLANE_DEVS, 16, 128), BF16),
            pltpu.VMEM((PLANE_DEVS, 16, 128), F32),
            pltpu.VMEM((PLANE, 8, 128), F32),
            pltpu.VMEM((32, 128), BF16),
            pltpu.VMEM((2, 32, 128), BF16),
            pltpu.VMEM((PLANE_DEVS, 16, 128), BF16),
            pltpu.VMEM((PLANE_DEVS, 16, 128), BF16),
            pltpu.VMEM((PAIRS, 128, 128), F32),
            pltpu.VMEM((128, HEADS * 128), BF16),
            pltpu.VMEM((8, 128, 128), F32),
            pltpu.VMEM((8, 128, 128), F32),
            pltpu.VMEM((8, 128, 128), F32),
            dma((9,)), dma((2, 8)), dma((2, 8)), dma((2, 8)), dma((2, 8)),
            dma((10,)), dma((10,)), dma((10,)), dma((10,)), dma, dma,
            dma((PLANE_DEVS,)), dma((PLANE_DEVS,)), dma((3,)), dma((3,)),
            dma((PLANE_DEVS,)), dma((PLANE_DEVS,)),
        ],
        compiler_params=pltpu.CompilerParams(
            collective_id=0, has_side_effects=True, vmem_limit_bytes=60 << 20
        ),
        name="hybrid_attention",
    )(*operands)
    return pl.pallas_call(
        hand_over,
        out_shape=tuple(jax.ShapeDtypeStruct(a.shape, a.dtype) for a in parts),
        in_specs=[anyw] * 2,
        out_specs=(anyw, anyw),
        scratch_shapes=[pltpu.VMEM(a.shape, a.dtype) for a in parts] + [dma((4,))],
        compiler_params=pltpu.CompilerParams(vmem_limit_bytes=60 << 20),
        name="results",
    )(*parts)


def solution(mesh):
    tokens = P(("outer", "inner"), None)
    return jax.shard_map(
        functools.partial(body, mesh.shape["outer"], feature_table()),
        mesh=mesh,
        in_specs=(tokens, tokens, tokens, P(), P(("outer", "inner")), tokens, tokens, tokens),
        out_specs=(tokens, tokens),
        check_vma=False,
    )
```

time: 46.7 us -> 42.6 us (0.912)
  local copies, waits for them, and re-layouts: 2.37 us -> 0 us
  Pallas kernels: 43.5 us -> 41.8 us
    pallas_call x1, Pallas kernels: 43.5 us -> 40.1 us  [body(): pl.pallas_call(functools.partial(kernel, outer), out_shape=(jax.ShapeDtyp...]
    unnamed x4 -> x0, local copies, waits for them, and re-layouts: 2.37 us -> none
    pallas_call x0 -> x1, Pallas kernels: none -> 1.78 us  [body(): pl.pallas_call(hand_over, out_shape=tuple((jax.ShapeDtypeStruct(a.shape,...]
where the time goes in v3:
time: 42.6 us; the launch traced here: 42.5 us
  Pallas kernels  41.8 us (98%)
  between operations  0.64 us (2%)
    pallas_call x1, Pallas kernels, body(): pl.pallas_call(functools.partial(kernel, outer), out_shape=(jax.ShapeDtyp...  40.1 us
    pallas_call x1, Pallas kernels, body(): pl.pallas_call(hand_over, out_shape=tuple((jax.ShapeDtypeStruct(a.shape,...  1.78 us

profile of v3, /device:TPU:1, one launch (start us, length us, event | category | flops | bytes accessed | tf_op | source)
XLA Modules:
  0.0 42.5 jit_solution(5935441400570505861)
XLA Ops:
  0.6 40.1 %hybrid_attention.1 = (bf16[128,640]{1,0:T(8,128)(2,1)}, bf16[128,1280]{1,0:T(8,128)(2,1)}) custom-call(bf16[110,128]{1,0:T(8,128)(2,1)} %bitcast.3, bf16[110,128]{1,0:T(8,128)(2,1)} %bitcast.4, bf16[128,640]{1,0:T(8,128)(2,1)} %bv_hbm.1, f32[640]{0:T(1024)} %gain_hbm.1, s32[1,128]{1,0:T(1,128)} %bitcast.5, f32[8,1280]{1,0:T(8,128)} %constant.2.clone.aux_hbm, ...), custom_call_target="tpu_custom_call" | custom-call | tf_op jit(solution)/shard_map/hybrid_attention/pallas_call | solution.py:481
  40.7 1.8 %results.1 = (bf16[128,640]{1,0:T(8,128)(2,1)}, bf16[128,1280]{1,0:T(8,128)(2,1)}) custom-call(bf16[128,640]{1,0:T(8,128)(2,1)} %get-tuple-element.4.based, bf16[128,1280]{1,0:T(8,128)(2,1)} %get-tuple-element.5.window), custom_call_target="tpu_custom_call" | custom-call | tf_op jit(solution)/shard_map/results/pallas_call | solution.py:521

commit v4 on v3

--- a/solution.py
+++ b/solution.py
@@ -69,6 +69,49 @@
     up = lax.rem(r + 1, outer)
     sib = x * 2 + (1 - c)
 
+    def to(dx, dc):
+        return lax.rem(x + dx, 4) * 2 + lax.rem(c + dc, 2)
+
+    plane_rows = [lax.rem(y + k, PLANE) for k in range(PLANE)]
+    plane_outer = [z * PLANE + k for k in plane_rows]
+    plane_inner = [lax.rem(i + k, 8) for k in range(8)]
+    others = [
+        (plane_rows[n // 8] * 8 + plane_inner[n % 8], plane_outer[n // 8], plane_inner[n % 8])
+        for n in range(1, PLANE_DEVS)
+    ]
+
+    def frm(dx, dc):
+        return lax.rem(x + 4 - dx, 4) * 2 + lax.rem(c + dc, 2)
+
+    def cols(ref, head):
+        return ref.at[:, pl.ds(pl.multiple_of(head * HEAD_DIM, HEAD_DIM), HEAD_DIM)]
+
+    def remote(src, dst, ss, rs, row, inner):
+        return pltpu.make_async_remote_copy(
+            src_ref=src, dst_ref=dst, send_sem=ss, recv_sem=rs,
+            device_id=(row, inner), device_id_type=MESH,
+        )
+
+    def arrived(dst, rs):
+        pltpu.make_async_copy(dst, dst, rs).wait()
+
+    sent = []
+
+    def send(src, dst, ss, rs, row, inner):
+        remote(src, dst, ss, rs, row, inner).start()
+        sent.append((src, ss))
+
+
+    barrier = pltpu.get_barrier_semaphore()
+    senders = [lax.rem(r + outer - 1, outer)]
+    senders += [lax.rem(r + outer - k * PLANE, outer) for k in (2, 1)]
+    for other in senders:
+        pl.semaphore_signal(barrier, inc=1, device_id=(other, i), device_id_type=MESH)
+    for _, row, inner in others[7:]:
+        pl.semaphore_signal(barrier, inc=1, device_id=(row, inner), device_id_type=MESH)
+    for dx, dc in ORDER:
+        pl.semaphore_signal(barrier, inc=1, device_id=(r, to(dx, dc)), device_id_type=MESH)
+
     loads = [
         pltpu.make_async_copy(src, dst, ld.at[n])
         for n, (src, dst) in enumerate(
@@ -80,49 +123,6 @@
     ]
     for load in loads:
         load.start()
-
-    def to(dx, dc):
-        return lax.rem(x + dx, 4) * 2 + lax.rem(c + dc, 2)
-
-    plane_rows = [lax.rem(y + k, PLANE) for k in range(PLANE)]
-    plane_outer = [z * PLANE + k for k in plane_rows]
-    plane_inner = [lax.rem(i + k, 8) for k in range(8)]
-    others = [
-        (plane_rows[n // 8] * 8 + plane_inner[n % 8], plane_outer[n // 8], plane_inner[n % 8])
-        for n in range(1, PLANE_DEVS)
-    ]
-
-    def frm(dx, dc):
-        return lax.rem(x + 4 - dx, 4) * 2 + lax.rem(c + dc, 2)
-
-    def cols(ref, head):
-        return ref.at[:, pl.ds(pl.multiple_of(head * HEAD_DIM, HEAD_DIM), HEAD_DIM)]
-
-    def remote(src, dst, ss, rs, row, inner):
-        return pltpu.make_async_remote_copy(
-            src_ref=src, dst_ref=dst, send_sem=ss, recv_sem=rs,
-            device_id=(row, inner), device_id_type=MESH,
-        )
-
-    def arrived(dst, rs):
-        pltpu.make_async_copy(dst, dst, rs).wait()
-
-    sent = []
-
-    def send(src, dst, ss, rs, row, inner):
-        remote(src, dst, ss, rs, row, inner).start()
-        sent.append((src, ss))
-
-    barrier = pltpu.get_barrier_semaphore()
-    for dx, dc in ORDER:
-        pl.semaphore_signal(barrier, inc=1, device_id=(r, to(dx, dc)), device_id_type=MESH)
-    senders = [lax.rem(r + outer - 1, outer)]
-    senders += [lax.rem(r + outer - k * PLANE, outer) for k in (1, 2)]
-    for other in senders:
-        pl.semaphore_signal(barrier, inc=1, device_id=(other, i), device_id_type=MESH)
-
-    for _, row, inner in others[7:]:
-        pl.semaphore_signal(barrier, inc=1, device_id=(row, inner), device_id_type=MESH)
 
 
     for load in loads[:4]:
@@ -204,6 +204,16 @@
 
     pass_on(range(1))
 
+    send_kv(range(5, 7))
+    arrived(cfw, rs_c)
+    kv[1, i] = cfw[c]
+    send(cfw.at[1 - c], kv.at[1, i], ss_prev.at[1, 0], rs_prev.at[1, i], r, sib)
+    pass_on(range(1, 5))
+    for n, (dx, dc) in enumerate(ORDER):
+        d = to(dx, dc)
+        send(sq.at[d], qb.at[i], ss_q.at[n], rs_q.at[i], r, d)
+
+    pass_on(range(5, 7))
     for place, _, _ in others:
         arrived(srecv.at[place], rs_s.at[place])
 
@@ -224,15 +234,6 @@
     for k in (1, 2):
         send(wsend, wrecv.at[k - 1], ss_w.at[k], rs_w.at[k], lax.rem(r + k * PLANE, outer), i)
 
-    send_kv(range(5, 7))
-    arrived(cfw, rs_c)
-    kv[1, i] = cfw[c]
-    send(cfw.at[1 - c], kv.at[1, i], ss_prev.at[1, 0], rs_prev.at[1, i], r, sib)
-    pass_on(range(1, 5))
-    for n, (dx, dc) in enumerate(ORDER):
-        d = to(dx, dc)
-        send(sq.at[d], qb.at[i], ss_q.at[n], rs_q.at[i], r, d)
-
     for n, (dx, dc) in enumerate(FAR):
         h = lax.rem(c + dc, 2)
         d = to(dx, dc)
@@ -249,7 +250,6 @@
                 cfw.at[h], kv.at[1, i], ss_prev.at[1, n + 1], rs_prev.at[1, i], r, d
             ).start()
 
-    pass_on(range(5, 7))
 
     xq = bq[...]
     inside = (own_cols == own_rows) & (lane <= row)

time: 42.6 us -> 42.2 us (level)
  no operation moved by 1% of the time
where the time goes in v4:
time: 42.2 us; the launch traced here: 42.1 us
  Pallas kernels  41.4 us (98%)
  between operations  0.64 us (2%)
    pallas_call x1, Pallas kernels, body(): pl.pallas_call(functools.partial(kernel, outer), out_shape=(jax.ShapeDtyp...  39.7 us
    pallas_call x1, Pallas kernels, body(): pl.pallas_call(hand_over, out_shape=tuple((jax.ShapeDtypeStruct(a.shape,...  1.78 us

profile of v4, /device:TPU:1, one launch (start us, length us, event | category | flops | bytes accessed | tf_op | source)
XLA Modules:
  0.0 42.1 jit_solution(10691378648882701734)
XLA Ops:
  0.6 39.7 %hybrid_attention.1 = (bf16[128,640]{1,0:T(8,128)(2,1)}, bf16[128,1280]{1,0:T(8,128)(2,1)}) custom-call(bf16[110,128]{1,0:T(8,128)(2,1)} %bitcast.3, bf16[110,128]{1,0:T(8,128)(2,1)} %bitcast.4, bf16[128,640]{1,0:T(8,128)(2,1)} %bv_hbm.1, f32[640]{0:T(1024)} %gain_hbm.1, s32[1,128]{1,0:T(1,128)} %bitcast.5, f32[8,1280]{1,0:T(8,128)} %constant.2.clone.aux_hbm, ...), custom_call_target="tpu_custom_call" | custom-call | tf_op jit(solution)/shard_map/hybrid_attention/pallas_call | solution.py:481
  40.3 1.8 %results.1 = (bf16[128,640]{1,0:T(8,128)(2,1)}, bf16[128,1280]{1,0:T(8,128)(2,1)}) custom-call(bf16[128,640]{1,0:T(8,128)(2,1)} %get-tuple-element.4.based, bf16[128,1280]{1,0:T(8,128)(2,1)} %get-tuple-element.5.window), custom_call_target="tpu_custom_call" | custom-call | tf_op jit(solution)/shard_map/results/pallas_call | solution.py:521

commit v5 on v4

--- a/solution.py
+++ b/solution.py
@@ -361,23 +361,17 @@
         def _():
             pltpu.make_async_copy(ob.at[j], cols(wout, i), ss_o.at[j]).start()
 
-    @pl.loop(0, 4)
-    def _(step):
-        arrived(kv.at[0, 7 - step], rs_prev.at[0, 7 - step])
-
-    @pl.loop(0, 4)
-    def _(step):
-        last_part(7 - step, 4)
-        finish(7 - step)
-
-    @pl.loop(0, 4)
-    def _(step):
-        arrived(kv.at[0, 3 - step], rs_prev.at[0, 3 - step])
-
-    @pl.loop(0, 4)
-    def _(step):
-        last_part(3 - step, 0)
-        finish(3 - step)
+    def finish_pair(first):
+        for slot in (first + 1, first):
+            arrived(kv.at[0, slot], rs_prev.at[0, slot])
+
+        @pl.loop(0, 2)
+        def _(step):
+            last_part(first + 1 - step, first)
+            finish(first + 1 - step)
+
+    for first in (6, 4, 2, 0):
+        finish_pair(first)
 
     arrived(qb.at[9 - c], rs_q.at[9 - c])
 

time: 42.2 us -> 42 us (level)
  no operation moved by 1% of the time
where the time goes in v5:
time: 42 us; the launch traced here: 41.9 us
  Pallas kernels  41.3 us (98%)
  between operations  0.64 us (2%)
    pallas_call x1, Pallas kernels, body(): pl.pallas_call(functools.partial(kernel, outer), out_shape=(jax.ShapeDtyp...  39.5 us
    pallas_call x1, Pallas kernels, body(): pl.pallas_call(hand_over, out_shape=tuple((jax.ShapeDtypeStruct(a.shape,...  1.78 us

profile of v5, /device:TPU:1, one launch (start us, length us, event | category | flops | bytes accessed | tf_op | source)
XLA Modules:
  0.0 41.9 jit_solution(10934768912798255972)
XLA Ops:
  0.6 39.5 %hybrid_attention.1 = (bf16[128,640]{1,0:T(8,128)(2,1)}, bf16[128,1280]{1,0:T(8,128)(2,1)}) custom-call(bf16[110,128]{1,0:T(8,128)(2,1)} %bitcast.3, bf16[110,128]{1,0:T(8,128)(2,1)} %bitcast.4, bf16[128,640]{1,0:T(8,128)(2,1)} %bv_hbm.1, f32[640]{0:T(1024)} %gain_hbm.1, s32[1,128]{1,0:T(1,128)} %bitcast.5, f32[8,1280]{1,0:T(8,128)} %constant.2.clone.aux_hbm, ...), custom_call_target="tpu_custom_call" | custom-call | tf_op jit(solution)/shard_map/hybrid_attention/pallas_call | solution.py:475
  40.1 1.8 %results.1 = (bf16[128,640]{1,0:T(8,128)(2,1)}, bf16[128,1280]{1,0:T(8,128)(2,1)}) custom-call(bf16[128,640]{1,0:T(8,128)(2,1)} %get-tuple-element.4.based, bf16[128,1280]{1,0:T(8,128)(2,1)} %get-tuple-element.5.window), custom_call_target="tpu_custom_call" | custom-call | tf_op jit(solution)/shard_map/results/pallas_call | solution.py:515
